TPU v7x, 512 devices: a whole 4x4x16 slice. The times are simulated.
512 devices in a mesh: dp: 16 (over z_lo, x), ctx: 32 (over z_hi, y, core).
Axes of the slice: x: 4, y: 4, z: 16 (z_hi: 4, z_lo: 4; z = z_hi * 4 + z_lo), core: 2. Of those that a mesh axis runs over, the one named last changes fastest.
Arguments:
- tokens: bfloat16 [16, 16384, 512], P('dp', 'ctx'), may hold values from -6 to 6
- cotangent: bfloat16 [16, 16384, 512], P('dp', 'ctx'), may hold values from -6 to 6
- gate_weight: bfloat16 [512, 512], replicated, may hold values from -0.25 to 0.25
- out_weight: bfloat16 [512, 512], replicated, may hold values from -0.25 to 0.25
- left_monarch_matrix: bfloat16 [32, 512, 512], P('ctx'), may hold values from -0.25 to 0.25
- right_factor: bfloat16 [512, 32, 32], P('ctx'), may hold values from -1 to 1
Outputs:
- output: bfloat16 [16, 16384, 512], P('dp', 'ctx')
- grad_tokens: bfloat16 [16, 16384, 512], P('dp', 'ctx')
- grad_gate: float32 [512, 512], P('ctx')
- grad_out: float32 [512, 512], P('ctx')
- grad_left: float32 [32, 512, 512], P('ctx')
- grad_right: float32 [512, 32, 32], P('ctx')
All inputs are finite; a program needn't handle non-finite values.
Results may differ from a plain program's by a relative error of at most 0.023.
Values may be sent and summed in bfloat16 or wider, within the bound.
No kernel may reach another device: no remote copies, remote signals or barrier semaphores. Data moves between devices by JAX's collectives and lax.ppermute only.
A program may use at most 64 MiB of HBM per device.

v0:
```python
import math

import jax
import jax.numpy as jnp
from jax import lax
from jax.sharding import PartitionSpec as P


def silu_parts(gate_pre):
    sigmoid_val = jax.nn.sigmoid(gate_pre)
    return (gate_pre * sigmoid_val, sigmoid_val * (1.0 + gate_pre * (1.0 - sigmoid_val)))


def per_device(tokens, cotangent, gate_weight, out_weight, left_monarch_matrix, right_factor):
    seq_tokens = tokens[0]
    seq_cotan = cotangent[0]
    tok_count = seq_tokens.shape[0]
    channels = seq_tokens.shape[1]
    blocks_here = left_monarch_matrix.shape[0]
    block_order = left_monarch_matrix.shape[1]
    seq_count = lax.axis_size("dp")
    ctx_count = lax.axis_size("ctx")
    weight_scale = 1.0 / math.sqrt(seq_count * ctx_count * tok_count)
    factor_scale = 1.0 / math.sqrt(seq_count * channels)
    token_blocks = seq_tokens.reshape(blocks_here, block_order, channels)
    initial_mixing = jnp.einsum(
        "nsg,ngt->nst", left_monarch_matrix, token_blocks, preferred_element_type=jnp.float32
    ).astype(jnp.bfloat16)
    first_moved = lax.all_to_all(initial_mixing, "ctx", split_axis=1, concat_axis=0, tiled=True)
    second_moved = jnp.einsum(
        "pkj,jpd->kpd", right_factor, first_moved, preferred_element_type=jnp.float32
    ).astype(jnp.bfloat16)
    second_mix = lax.all_to_all(second_moved, "ctx", split_axis=0, concat_axis=1, tiled=True)
    mixed_rows = second_mix.reshape(tok_count, channels).astype(jnp.float32)
    gate_pre = jnp.dot(seq_tokens, gate_weight, preferred_element_type=jnp.float32)
    activated, slope = silu_parts(gate_pre)
    hidden = (mixed_rows * activated).astype(jnp.bfloat16)
    result = jnp.dot(hidden, out_weight, preferred_element_type=jnp.float32).astype(jnp.bfloat16)
    grad_hidden = jnp.dot(seq_cotan, out_weight.T, preferred_element_type=jnp.float32)
    grad_second = (grad_hidden * activated).astype(jnp.bfloat16)
    grad_gate_pre = (grad_hidden * mixed_rows * slope).astype(jnp.bfloat16)
    grad_blocks = grad_second.reshape(blocks_here, block_order, channels)
    grad_moved = lax.all_to_all(grad_blocks, "ctx", split_axis=1, concat_axis=0, tiled=True)
    first_grad_moved = jnp.einsum(
        "pkj,kpd->jpd", right_factor, grad_moved, preferred_element_type=jnp.float32
    ).astype(jnp.bfloat16)
    term_right = jnp.einsum(
        "kpd,jpd->pkj", grad_moved, first_moved, preferred_element_type=jnp.float32
    )
    term_out = jnp.dot(hidden.T, seq_cotan, preferred_element_type=jnp.float32)
    term_gate = jnp.dot(seq_tokens.T, grad_gate_pre, preferred_element_type=jnp.float32)
    through_gate = jnp.dot(grad_gate_pre, gate_weight.T, preferred_element_type=jnp.float32)
    initial_gradient = lax.all_to_all(
        first_grad_moved, "ctx", split_axis=0, concat_axis=1, tiled=True
    )
    left_contribution = jnp.einsum(
        "xam,xom->xao", initial_gradient, token_blocks, preferred_element_type=jnp.float32
    )
    after_left_factor = jnp.einsum(
        "hfg,hfe->hge", left_monarch_matrix, initial_gradient, preferred_element_type=jnp.float32
    ).reshape(tok_count, channels)
    grad_seq = (after_left_factor + through_gate).astype(jnp.bfloat16)
    whole_gate, whole_out = lax.psum((term_gate, term_out), ("dp", "ctx"))
    share_rows = channels // ctx_count
    first_row = lax.axis_index("ctx") * share_rows
    sum_gate = lax.dynamic_slice_in_dim(whole_gate, first_row, share_rows, 0)
    sum_out = lax.dynamic_slice_in_dim(whole_out, first_row, share_rows, 0)
    sum_left, sum_right = (
        lax.psum(left_contribution.astype(jnp.bfloat16), "dp").astype(jnp.float32),
        lax.psum(term_right.astype(jnp.bfloat16), "dp").astype(jnp.float32),
    )
    return (
        result[None],
        grad_seq[None],
        sum_gate * weight_scale,
        sum_out * weight_scale,
        sum_left * factor_scale,
        sum_right * factor_scale,
    )


def solution(mesh):
    return jax.shard_map(
        per_device,
        mesh=mesh,
        in_specs=(
            P("dp", "ctx", None),
            P("dp", "ctx", None),
            P(),
            P(),
            P("ctx", None, None),
            P("ctx", None, None),
        ),
        out_specs=(
            P("dp", "ctx", None),
            P("dp", "ctx", None),
            P("ctx", None),
            P("ctx", None),
            P("ctx", None, None),
            P("ctx", None, None),
        ),
        check_vma=False,
    )
```

profile of v0, /device:TPU:16, one launch (start us, length us, event | category | flops | bytes accessed | tf_op | source)
XLA Modules:
  0.0 903.8 jit_solution(3650374437374868183)
XLA Ops:
  8.0 1.0 copy-done
  9.0 1.5 fusion.4
  10.5 0.8 copy.74
  11.9 3.8 reduce
  16.1 45.1 %all_to_all.42 = bf16[32,2,4096]{2,1,0:T(2,128)(2,1)S(1)} all-to-all(bf16[32,2,4096]{2,1,0:T(2,128)(2,1)S(1)} %reshape.57), channel_id=1, replica_groups=mesh['dp'=16,'ctx'=32] {'ctx'}, dimensions={0} | all-to-all | bytes 1048576 | tf_op jit(solution)/shard_map/all_to_all | solution.py:29
  61.2 0.5 reshape.58
  61.9 0.8 copy-done.10
  63.1 1.1 copy.46
  64.2 11.3 %all-to-all-start.1 = ((bf16[32,16,512]{2,1,0:T(8,128)(2,1)}), bf16[32,16,512]{2,1,0:T(8,128)(2,1)}, u32[]{:S(2)}, u32[]{:S(2)}) async-start(bf16[32,16,512]{2,1,0:T(8,128)(2,1)} %copy.46), calls=%async_computation.1 | async-start | bytes 1048576 | tf_op jit(solution)/shard_map/all_to_all | solution.py:33
  76.0 26.7 %all-to-all-done.1 = bf16[32,16,512]{2,1,0:T(8,128)(2,1)} async-done(((bf16[32,16,512]{2,1,0:T(8,128)(2,1)}), bf16[32,16,512]{2,1,0:T(8,128)(2,1)}, u32[]{:S(2)}, u32[]{:S(2)}) %all-to-all-start.1) | async-done | bytes 524320 | tf_op jit(solution)/shard_map/all_to_all | solution.py:33
  102.7 3.1 fusion.9
  105.8 0.8 copy.73
  106.6 3.8 reduce.1
  110.8 37.5 %all_to_all.43 = bf16[32,2,4096]{2,1,0:T(2,128)(2,1)S(1)} all-to-all(bf16[32,2,4096]{2,1,0:T(2,128)(2,1)S(1)} %reshape.59), channel_id=1, replica_groups=mesh['dp'=16,'ctx'=32] {'ctx'}, dimensions={0} | all-to-all | bytes 1048576 | tf_op jit(solution)/shard_map/all_to_all | solution.py:43
  149.4 1.1 copy.50
  150.5 11.8 %all-to-all-start.3 = ((bf16[32,16,512]{2,1,0:T(8,128)(2,1)}), bf16[32,16,512]{2,1,0:T(8,128)(2,1)S(1)}, u32[]{:S(2)}, u32[]{:S(2)}) async-start(bf16[32,16,512]{2,1,0:T(8,128)(2,1)} %copy.50), calls=%async_computation.3 | async-start | bytes 1048576 | tf_op jit(solution)/shard_map/all_to_all | solution.py:53
  162.4 1.4 convolution_bitcast_fusion
  163.9 1.5 fusion.12
  165.4 1.0 copy-done.6
  166.4 1.2 fusion.5
  167.6 478.0 %all-reduce.6.cloned.1.call-done = (f32[512,512]{0,1:T(8,128)}, f32[512,512]{0,1:T(8,128)}) async-done(((f32[512,512]{0,1:T(8,128)}, f32[512,512]{0,1:T(8,128)}), (f32[512,512]{0,1:T(8,128)}, f32[512,512]{0,1:T(8,128)})) %all-reduce.6.cloned.1.call-update) | async-done | bytes 2097168 | tf_op jit(solution)/shard_map/psum | solution.py:63
  645.6 1.2 dynamic-slice_multiply_fusion
  646.9 0.7 copy.56
  647.6 0.7 copy.57
  648.3 0.7 convolution_convert_fusion.5
  649.0 76.1 %psum.31 = bf16[16,32,32]{2,1,0:T(8,128)(2,1)S(1)} all-reduce(bf16[16,32,32]{2,1,0:T(8,128)(2,1)S(1)} %convolution_convert_fusion.5), channel_id=1, replica_groups=mesh['dp'=16,'ctx'=32] {'dp'}, use_global_device_ids=true, to_apply=%region_3.0 | all-reduce | flops 16384 | bytes 65536 | tf_op jit(solution)/shard_map/psum | solution.py:70
  725.1 1.3 fusion.6
  726.3 0.7 convert_multiply_fusion.3
  727.9 0.6 copy-done.4
  729.1 1.0 copy.55
  730.1 164.0 %all-reduce.4.cloned.1.call-done = bf16[1,512,512]{2,1,0:T(8,128)(2,1)} async-done(((bf16[1,512,512]{2,1,0:T(8,128)(2,1)}), bf16[1,512,512]{2,1,0:T(8,128)(2,1)}) %all-reduce.4.cloned.1.call-update) | async-done | bytes 524304 | tf_op jit(solution)/shard_map/psum | solution.py:69
  894.2 2.2 convert_multiply_fusion.2
  (34 shorter events, 5.1 us)
Async XLA Ops:
  8.0 1.0 copy-start
  61.7 0.9 copy-start.10
  64.2 11.3 %copy-start.1 = (bf16[512,512]{1,0:T(8,128)(2,1)S(1)}, bf16[512,512]{1,0:T(8,128)(2,1)}, u32[]{:S(2)}) copy-start(bf16[512,512]{1,0:T(8,128)(2,1)} %param.9) | copy-start | bytes 1572868
  64.2 11.3 %copy-start.7 = (bf16[1,512,512]{2,1,0:T(8,128)(2,1)S(1)}, bf16[1,512,512]{2,1,0:T(8,128)(2,1)}, u32[]{:S(2)}) copy-start(bf16[1,512,512]{2,1,0:T(8,128)(2,1)} %param.7) | copy-start | bytes 1572868
  64.2 38.5 %all-to-all-start.1 = ((bf16[32,16,512]{2,1,0:T(8,128)(2,1)}), bf16[32,16,512]{2,1,0:T(8,128)(2,1)}, u32[]{:S(2)}, u32[]{:S(2)}) async-start(bf16[32,16,512]{2,1,0:T(8,128)(2,1)} %copy.46), calls=%async_computation.1 | async-start | bytes 1048576 | tf_op jit(solution)/shard_map/all_to_all | solution.py:33
  150.5 11.8 %copy-start.3 = (bf16[512,512]{1,0:T(8,128)(2,1)S(1)}, bf16[512,512]{1,0:T(8,128)(2,1)}, u32[]{:S(2)}) copy-start(bf16[512,512]{1,0:T(8,128)(2,1)} %get-tuple-element.32) | copy-start | bytes 1572868
  150.5 574.5 %all-to-all-start.3 = ((bf16[32,16,512]{2,1,0:T(8,128)(2,1)}), bf16[32,16,512]{2,1,0:T(8,128)(2,1)S(1)}, u32[]{:S(2)}, u32[]{:S(2)}) async-start(bf16[32,16,512]{2,1,0:T(8,128)(2,1)} %copy.50), calls=%async_computation.3 | async-start | bytes 1048576 | tf_op jit(solution)/shard_map/all_to_all | solution.py:53
  162.3 483.3 %all-reduce.6.cloned.1.call-start = ((), (), s32[]{:S(2)}) async-start(), calls=%async_computation.5 | async-start | bytes 4194304 | tf_op jit(solution)/shard_map/psum | solution.py:63
  162.4 1.5 copy-start.5
  162.4 1.4 copy-start.8
  165.3 1.0 copy-start.6
  165.4 728.8 %all-reduce.4.cloned.1.call-start = ((), (), s32[]{:S(2)}) async-start(), calls=%async_computation.4 | async-start | bytes 1048576 | tf_op jit(solution)/shard_map/psum | solution.py:69
  726.3 1.1 copy-start.2
  727.5 1.0 copy-start.4
  727.5 1.2 copy-start.9
Sparse Core Ops, SparseCore 0:
  169.2 476.4 all-reduce.5
Sparse Core Ops, SparseCore 1:
  726.4 167.7 all-reduce.3
where the time goes:
time: 905 us; the launch traced here: 904 us
  waiting for transfers between devices  669 us (74%)
  blocking collectives  159 us (18%)
  starting transfers between devices  23.2 us (3%)
  between operations  15.7 us (2%)
  matrix products  13 us (1%)
  local copies, waits for them, and re-layouts  12.7 us (1%)
  other arithmetic  11.8 us (1%)
    psum x1, waiting for transfers between devices, per_device(): whole_gate, whole_out = lax.psum((term_gate, term_out), ('dp', 'ctx'))  478 us
    psum x1, waiting for transfers between devices, per_device(): lax.psum(left_contribution.astype(jnp.bfloat16), 'dp').astype(jnp.float32)  164 us
    psum x1, blocking collectives, per_device(): lax.psum(term_right.astype(jnp.bfloat16), 'dp').astype(jnp.float32)  76.1 us
    all_to_all x1, blocking collectives, per_device(): lax.all_to_all(initial_mixing, 'ctx', split_axis=1, concat_axis=0, tiled=...  45.1 us
    all_to_all x1, blocking collectives, per_device(): lax.all_to_all(grad_blocks, 'ctx', split_axis=1, concat_axis=0, tiled=True)  37.5 us
    all_to_all x1, waiting for transfers between devices, per_device(): lax.all_to_all(second_moved, 'ctx', split_axis=0, concat_axis=1, tiled=True)  26.7 us
  transfers between devices with their start and end apart: 4, of which 3 were waited for; matrix products, arithmetic and copies ran while one was open for 1% of the time, Pallas kernels for 0%

commit v1 on v0

v1 whole, which is shorter than its diff:
```python
import math

import jax
import jax.numpy as jnp
from jax import lax
from jax.sharding import Mesh, PartitionSpec as P

DP = ("zl", "x")
CTX = ("zh", "y", "c")
BF = jnp.bfloat16
F32 = jnp.float32


def mm(a, b):
    return jnp.dot(a, b, preferred_element_type=F32)


def mm_t(a, b):
    return lax.dot_general(a, b, (((1,), (1,)), ((), ())), preferred_element_type=F32)


def mm_tl(a, b):
    return lax.dot_general(a, b, (((0,), (0,)), ((), ())), preferred_element_type=F32)


def swap(blocks, axes):
    return lax.all_to_all(blocks, axes, 0, 0, tiled=True)


def per_device(tokens, cotangent, gate_weight, out_weight, left_matrix, right_factor):
    x = tokens[0]
    cot = cotangent[0]
    left = left_matrix[0]
    tok, ch = x.shape
    pos, nb, _ = right_factor.shape
    seqs = lax.axis_size(DP)
    ctx = lax.axis_size(CTX)
    weight_scale = 1.0 / math.sqrt(seqs * ctx * tok)
    factor_scale = 1.0 / math.sqrt(seqs * ch)

    first_mix = mm(left, x).astype(BF)
    first_moved = swap(first_mix.reshape(nb, pos, ch), CTX)

    gate_pre = mm(x, gate_weight)
    grad_hidden = mm_t(cot, out_weight)
    sig = jax.nn.sigmoid(gate_pre)
    activated = gate_pre * sig
    slope = sig * (1.0 + gate_pre * (1.0 - sig))
    grad_second = (grad_hidden * activated).astype(BF)
    grad_moved = swap(grad_second.reshape(nb, pos, ch), CTX)

    same = jnp.eye(pos, dtype=BF)
    wide = (right_factor.transpose(1, 0, 2)[:, :, :, None] * same[None, :, None, :]).reshape(nb * pos, nb * pos)

    first_flat = first_moved.reshape(nb * pos, ch)
    second_moved = mm(wide, first_flat).astype(BF)
    second_mix = swap(second_moved.reshape(nb, pos, ch), CTX)

    first_grad_moved = mm_tl(wide, grad_moved.reshape(nb * pos, ch)).astype(BF)
    initial_gradient = swap(first_grad_moved.reshape(nb, pos, ch), CTX).reshape(tok, ch)

    term_right = jnp.einsum("kpd,jpd->pkj", grad_moved, first_moved, preferred_element_type=F32)

    mixed = second_mix.reshape(tok, ch).astype(F32)
    hidden = (mixed * activated).astype(BF)
    grad_gate_pre = (grad_hidden * mixed * slope).astype(BF)
    result = mm(hidden, out_weight).astype(BF)
    through_gate = mm_t(grad_gate_pre, gate_weight)
    term_gate = mm_tl(x, grad_gate_pre).astype(BF)
    term_out = mm_tl(hidden, cot).astype(BF)

    share = ch // ctx
    zh = lax.axis_size("zh")
    yc = lax.axis_size(("y", "c"))

    def by_yc(term):
        return term.reshape(zh, yc, share, ch).transpose(1, 0, 2, 3)

    terms = jnp.stack([by_yc(term_gate), by_yc(term_out)], 2)
    terms = swap(terms.reshape(yc, zh * 2 * share, ch), ("y", "c"))
    terms = terms.astype(F32).sum(0).astype(BF).reshape(zh, 2 * share, ch)
    terms = swap(terms, "zh").astype(F32).sum(0).astype(BF)
    small = jnp.concatenate([terms, term_right.astype(BF).reshape(-1, ch)], 0)
    small = lax.all_gather(small, DP, axis=0).astype(F32).sum(0)
    sum_gate = small[:share]
    sum_out = small[share : 2 * share]
    sum_right = small[2 * share :].reshape(pos, nb, nb)

    term_left = mm_t(initial_gradient, x).astype(BF)
    part = swap(term_left.reshape(seqs, tok // seqs, tok), DP).astype(F32).sum(0).astype(BF)
    spread = jnp.broadcast_to(part[None], (seqs,) + part.shape)
    sum_left = swap(spread, DP).reshape(1, tok, tok).astype(F32)

    grad_tokens = (mm_tl(left, initial_gradient) + through_gate).astype(BF)

    return (
        result[None],
        grad_tokens[None],
        sum_gate * weight_scale,
        sum_out * weight_scale,
        sum_left * factor_scale,
        sum_right * factor_scale,
    )


def solution(mesh):
    fine = Mesh(mesh.devices.reshape(4, 4, 4, 4, 2), DP + CTX)
    tok = P(DP, CTX, None)
    own = P(CTX, None, None)
    return jax.shard_map(
        per_device,
        mesh=fine,
        in_specs=(tok, tok, P(), P(), own, own),
        out_specs=(tok, tok, P(CTX, None), P(CTX, None), own, own),
        check_vma=False,
    )
```

time: 905 us -> 322 us (0.36)
  the two profiles are of different devices: /device:TPU:16 before, /device:TPU:8 now
where the time goes in v1:
time: 322 us; the launch traced here: 321 us
  waiting for transfers between devices  187 us (58%)
  starting transfers between devices  79.1 us (25%)
  matrix products  17.8 us (6%)
  between operations  14.2 us (4%)
  local copies, waits for them, and re-layouts  12.6 us (4%)
  other arithmetic  9.65 us (3%)
    all_to_all x8, waiting for transfers between devices, swap(): return lax.all_to_all(blocks, axes, 0, 0, tiled=True)  125 us
    all_to_all x8, starting transfers between devices, swap(): return lax.all_to_all(blocks, axes, 0, 0, tiled=True)  79.1 us
    all_gather x1, waiting for transfers between devices, per_device(): small = lax.all_gather(small, DP, axis=0).astype(F32).sum(0)  62.1 us
    mul x1, local copies, waits for them, and re-layouts, per_device(): right_factor.transpose(1, 0, 2)[:, :, :, None] * same[None, :, None, :]  7.89 us
    dot_general x4, matrix products, mm(): return jnp.dot(a, b, preferred_element_type=F32)  7.56 us
  transfers between devices with their start and end apart: 9, of which 8 were waited for; matrix products, arithmetic and copies ran while one was open for 10% of the time, Pallas kernels for 0%

profile of v1, /device:TPU:8, one launch (start us, length us, event | category | flops | bytes accessed | tf_op | source)
XLA Modules:
  0.0 320.8 jit_solution(947481564701257375)
XLA Ops:
  7.2 2.5 convolution_convert_fusion.6
  9.7 18.3 %all-to-all-start = ((bf16[32,16,512]{2,1,0:T(8,128)(2,1)}), bf16[32,16,512]{2,1,0:T(8,128)(2,1)S(1)}, u32[]{:S(2)}, u32[]{:S(2)}) async-start(bf16[32,16,512]{2,1,0:T(8,128)(2,1)} %bitcast.3), calls=%async_computation | async-start | bytes 1048576 | tf_op jit(solution)/shard_map/all_to_all | solution.py:27
  28.0 1.0 copy.33
  29.0 3.9 %broadcast_multiply_fusion = bf16[32,16,32,16]{3,2,1,0:T(8,128)(2,1)} fusion(bf16[16,16]{1,0:T(8,128)(2,1)S(1)} %fusion.19, bf16[32,16,32]{2,1,0:T(8,128)(2,1)S(1)} %copy.33), kind=kLoop, calls=%fused_computation.1 | loop fusion | flops 262144 | bytes 557568 | tf_op jit(solution)/shard_map/mul | solution.py:53
  32.9 7.9 %mul.83 = bf16[512,512]{1,0:T(8,128)(2,1)S(1)} reshape(bf16[32,16,32,16]{3,2,1,0:T(8,128)(2,1)} %broadcast_multiply_fusion) | data formatting | bytes 1048576 | tf_op jit(solution)/shard_map/mul | solution.py:53
  40.8 15.1 %all-to-all-done = bf16[32,16,512]{2,1,0:T(8,128)(2,1)S(1)} async-done(((bf16[32,16,512]{2,1,0:T(8,128)(2,1)}), bf16[32,16,512]{2,1,0:T(8,128)(2,1)S(1)}, u32[]{:S(2)}, u32[]{:S(2)}) %all-to-all-start) | async-done | bytes 524320 | tf_op jit(solution)/shard_map/all_to_all | solution.py:27
  55.9 1.2 convolution_convert_fusion.5
  57.1 10.4 %all-to-all-start.1 = ((bf16[32,16,512]{2,1,0:T(8,128)(2,1)}), bf16[32,16,512]{2,1,0:T(8,128)(2,1)}, u32[]{:S(2)}, u32[]{:S(2)}) async-start(bf16[32,16,512]{2,1,0:T(8,128)(2,1)} %bitcast.5), calls=%async_computation.1 | async-start | bytes 1048576 | tf_op jit(solution)/shard_map/all_to_all | solution.py:27
  67.5 1.4 fusion.12
  68.9 25.9 %all-to-all-done.1 = bf16[32,16,512]{2,1,0:T(8,128)(2,1)} async-done(((bf16[32,16,512]{2,1,0:T(8,128)(2,1)}), bf16[32,16,512]{2,1,0:T(8,128)(2,1)}, u32[]{:S(2)}, u32[]{:S(2)}) %all-to-all-start.1) | async-done | bytes 524320 | tf_op jit(solution)/shard_map/all_to_all | solution.py:27
  94.8 3.0 fusion.5
  97.8 11.0 %all-to-all-start.2 = ((bf16[32,16,512]{2,1,0:T(8,128)(2,1)}), bf16[32,16,512]{2,1,0:T(8,128)(2,1)S(1)}, u32[]{:S(2)}, u32[]{:S(2)}) async-start(bf16[32,16,512]{2,1,0:T(8,128)(2,1)} %bitcast.81), calls=%async_computation.2 | async-start | bytes 1048576 | tf_op jit(solution)/shard_map/all_to_all | solution.py:27
  109.8 1.1 pad_maximum_fusion
  110.9 24.5 %all-to-all-done.2 = bf16[32,16,512]{2,1,0:T(8,128)(2,1)S(1)} async-done(((bf16[32,16,512]{2,1,0:T(8,128)(2,1)}), bf16[32,16,512]{2,1,0:T(8,128)(2,1)S(1)}, u32[]{:S(2)}, u32[]{:S(2)}) %all-to-all-start.2) | async-done | bytes 524320 | tf_op jit(solution)/shard_map/all_to_all | solution.py:27
  136.2 6.2 %all-to-all-start.4 = ((bf16[8,128,512]{2,1,0:T(8,128)(2,1)}), bf16[8,128,512]{2,1,0:T(8,128)(2,1)S(1)}, u32[]{:S(2)}, u32[]{:S(2)}) async-start(bf16[8,128,512]{2,1,0:T(8,128)(2,1)} %bitcast.75), calls=%async_computation.4 | async-start | bytes 2097152 | tf_op jit(solution)/shard_map/all_to_all | solution.py:27
  142.4 2.3 convolution_convert_fusion.3
  144.7 12.2 %all-to-all-done.4 = bf16[8,128,512]{2,1,0:T(8,128)(2,1)S(1)} async-done(((bf16[8,128,512]{2,1,0:T(8,128)(2,1)}), bf16[8,128,512]{2,1,0:T(8,128)(2,1)S(1)}, u32[]{:S(2)}, u32[]{:S(2)}) %all-to-all-start.4) | async-done | bytes 1048608 | tf_op jit(solution)/shard_map/all_to_all | solution.py:27
  156.9 9.7 %all-to-all-start.3 = ((bf16[32,16,512]{2,1,0:T(8,128)(2,1)}), bf16[32,16,512]{2,1,0:T(8,128)(2,1)S(1)}, u32[]{:S(2)}, u32[]{:S(2)}) async-start(bf16[32,16,512]{2,1,0:T(8,128)(2,1)} %bitcast.82), calls=%async_computation.3 | async-start | bytes 1048576 | tf_op jit(solution)/shard_map/all_to_all | solution.py:27
  167.5 23.2 %all-to-all-done.3 = bf16[32,16,512]{2,1,0:T(8,128)(2,1)S(1)} async-done(((bf16[32,16,512]{2,1,0:T(8,128)(2,1)}), bf16[32,16,512]{2,1,0:T(8,128)(2,1)S(1)}, u32[]{:S(2)}, u32[]{:S(2)}) %all-to-all-start.3) | async-done | bytes 524320 | tf_op jit(solution)/shard_map/all_to_all | solution.py:27
  190.7 4.4 %all-to-all-start.5 = ((bf16[4,32,512]{2,1,0:T(8,128)(2,1)}), bf16[4,32,512]{2,1,0:T(8,128)(2,1)S(1)}, u32[]{:S(2)}, u32[]{:S(2)}) async-start(bf16[4,32,512]{2,1,0:T(8,128)(2,1)} %bitcast.24), calls=%async_computation.5 | async-start | bytes 262144 | tf_op jit(solution)/shard_map/all_to_all | solution.py:27
  195.2 1.3 convolution_convert_fusion
  196.4 12.4 %all-to-all-done.5 = bf16[4,32,512]{2,1,0:T(8,128)(2,1)S(1)} async-done(((bf16[4,32,512]{2,1,0:T(8,128)(2,1)}), bf16[4,32,512]{2,1,0:T(8,128)(2,1)S(1)}, u32[]{:S(2)}, u32[]{:S(2)}) %all-to-all-start.5) | async-done | bytes 131104 | tf_op jit(solution)/shard_map/all_to_all | solution.py:27
  208.8 14.6 %all-to-all-start.6 = ((bf16[16,32,512]{2,1,0:T(8,128)(2,1)}), bf16[16,32,512]{2,1,0:T(8,128)(2,1)S(1)}, u32[]{:S(2)}, u32[]{:S(2)}) async-start(bf16[16,32,512]{2,1,0:T(8,128)(2,1)} %bitcast.26), calls=%async_computation.6 | async-start | bytes 1048576 | tf_op jit(solution)/shard_map/all_to_all | solution.py:27
  223.5 1.9 convolution_convert_fusion.7
  226.2 12.0 %all-to-all-done.6 = bf16[16,32,512]{2,1,0:T(8,128)(2,1)S(1)} async-done(((bf16[16,32,512]{2,1,0:T(8,128)(2,1)}), bf16[16,32,512]{2,1,0:T(8,128)(2,1)S(1)}, u32[]{:S(2)}, u32[]{:S(2)}) %all-to-all-start.6) | async-done | bytes 524320 | tf_op jit(solution)/shard_map/all_to_all | solution.py:27
  238.3 0.8 broadcast_in_dim.16
  239.1 4.4 %all-to-all-start.7 = ((bf16[16,32,512]{2,1,0:T(8,128)(2,1)}), bf16[16,32,512]{2,1,0:T(8,128)(2,1)S(1)}, u32[]{:S(2)}, u32[]{:S(2)}) async-start(bf16[16,32,512]{2,1,0:T(8,128)(2,1)} %broadcast_in_dim.16), calls=%async_computation.7 | async-start | bytes 1048576 | tf_op jit(solution)/shard_map/all_to_all | solution.py:27
  243.5 2.4 fusion.2
  246.0 62.1 %all-gather.3.cloned.1.call-done = bf16[1024,512]{1,0:T(8,128)(2,1)} async-done(((bf16[64,512]{1,0:T(8,128)(2,1)}), bf16[1024,512]{1,0:T(8,128)(2,1)}) %all-gather.3.cloned.1.call-update) | async-done | bytes 1048592 | tf_op jit(solution)/shard_map/all_gather | solution.py:84
  308.0 1.4 convert_reduce_fusion
  311.8 1.0 copy.39
  312.9 1.1 convert_multiply_fusion.2
  (35 shorter events, 6.0 us)
Async XLA Ops:
  7.2 87.7 %copy-start = (bf16[1,512,512]{2,1,0:T(8,128)(2,1)S(1)}, bf16[1,512,512]{2,1,0:T(8,128)(2,1)}, u32[]{:S(2)}) copy-start(bf16[1,512,512]{2,1,0:T(8,128)(2,1)} %param.7) | copy-start | bytes 1572868
  9.7 46.2 %all-to-all-start = ((bf16[32,16,512]{2,1,0:T(8,128)(2,1)}), bf16[32,16,512]{2,1,0:T(8,128)(2,1)S(1)}, u32[]{:S(2)}, u32[]{:S(2)}) async-start(bf16[32,16,512]{2,1,0:T(8,128)(2,1)} %bitcast.3), calls=%async_computation | async-start | bytes 1048576 | tf_op jit(solution)/shard_map/all_to_all | solution.py:27
  32.9 34.6 %copy-start.1 = (bf16[1,512,512]{2,1,0:T(8,128)(2,1)S(1)}, bf16[1,512,512]{2,1,0:T(8,128)(2,1)}, u32[]{:S(2)}) copy-start(bf16[1,512,512]{2,1,0:T(8,128)(2,1)} %param.6) | copy-start | bytes 1572868
  32.9 34.7 %copy-start.4 = (bf16[512,512]{1,0:T(8,128)(2,1)S(1)}, bf16[512,512]{1,0:T(8,128)(2,1)}, u32[]{:S(2)}) copy-start(bf16[512,512]{1,0:T(8,128)(2,1)} %param.8) | copy-start | bytes 1572868
  32.9 62.0 %copy-start.6 = (bf16[512,512]{1,0:T(8,128)(2,1)S(1)}, bf16[512,512]{1,0:T(8,128)(2,1)}, u32[]{:S(2)}) copy-start(bf16[512,512]{1,0:T(8,128)(2,1)} %param.9) | copy-start | bytes 1572868
  55.9 13.0 %copy-start.2 = (bf16[32,16,512]{2,1,0:T(8,128)(2,1)}, bf16[32,16,512]{2,1,0:T(8,128)(2,1)S(1)}, u32[]{:S(2)}) copy-start(bf16[32,16,512]{2,1,0:T(8,128)(2,1)S(1)} %all-to-all-done) | copy-start | bytes 1572868
  57.1 37.7 %all-to-all-start.1 = ((bf16[32,16,512]{2,1,0:T(8,128)(2,1)}), bf16[32,16,512]{2,1,0:T(8,128)(2,1)}, u32[]{:S(2)}, u32[]{:S(2)}) async-start(bf16[32,16,512]{2,1,0:T(8,128)(2,1)} %bitcast.5), calls=%async_computation.1 | async-start | bytes 1048576 | tf_op jit(solution)/shard_map/all_to_all | solution.py:27
  97.8 13.1 %copy-start.7 = (bf16[512,512]{1,0:T(8,128)(2,1)}, bf16[512,512]{1,0:T(8,128)(2,1)S(1)}, u32[]{:S(2)}) copy-start(bf16[512,512]{1,0:T(8,128)(2,1)S(1)} %get-tuple-element.32) | copy-start | bytes 1572868
  97.8 37.6 %all-to-all-start.2 = ((bf16[32,16,512]{2,1,0:T(8,128)(2,1)}), bf16[32,16,512]{2,1,0:T(8,128)(2,1)S(1)}, u32[]{:S(2)}, u32[]{:S(2)}) async-start(bf16[32,16,512]{2,1,0:T(8,128)(2,1)} %bitcast.81), calls=%async_computation.2 | async-start | bytes 1048576 | tf_op jit(solution)/shard_map/all_to_all | solution.py:27
  135.4 0.8 copy-start.8
  136.2 20.7 %all-to-all-start.4 = ((bf16[8,128,512]{2,1,0:T(8,128)(2,1)}), bf16[8,128,512]{2,1,0:T(8,128)(2,1)S(1)}, u32[]{:S(2)}, u32[]{:S(2)}) async-start(bf16[8,128,512]{2,1,0:T(8,128)(2,1)} %bitcast.75), calls=%async_computation.4 | async-start | bytes 2097152 | tf_op jit(solution)/shard_map/all_to_all | solution.py:27
  156.9 33.8 %all-to-all-start.3 = ((bf16[32,16,512]{2,1,0:T(8,128)(2,1)}), bf16[32,16,512]{2,1,0:T(8,128)(2,1)S(1)}, u32[]{:S(2)}, u32[]{:S(2)}) async-start(bf16[32,16,512]{2,1,0:T(8,128)(2,1)} %bitcast.82), calls=%async_computation.3 | async-start | bytes 1048576 | tf_op jit(solution)/shard_map/all_to_all | solution.py:27
  190.7 18.1 %all-to-all-start.5 = ((bf16[4,32,512]{2,1,0:T(8,128)(2,1)}), bf16[4,32,512]{2,1,0:T(8,128)(2,1)S(1)}, u32[]{:S(2)}, u32[]{:S(2)}) async-start(bf16[4,32,512]{2,1,0:T(8,128)(2,1)} %bitcast.24), calls=%async_computation.5 | async-start | bytes 262144 | tf_op jit(solution)/shard_map/all_to_all | solution.py:27
  208.8 102.1 %copy-start.3 = (bf16[1,512,512]{2,1,0:T(8,128)(2,1)S(1)}, bf16[1,512,512]{2,1,0:T(8,128)(2,1)}, u32[]{:S(2)}) copy-start(bf16[1,512,512]{2,1,0:T(8,128)(2,1)} %param.10) | copy-start | bytes 1572868
  208.8 29.4 %all-to-all-start.6 = ((bf16[16,32,512]{2,1,0:T(8,128)(2,1)}), bf16[16,32,512]{2,1,0:T(8,128)(2,1)S(1)}, u32[]{:S(2)}, u32[]{:S(2)}) async-start(bf16[16,32,512]{2,1,0:T(8,128)(2,1)} %bitcast.26), calls=%async_computation.6 | async-start | bytes 1048576 | tf_op jit(solution)/shard_map/all_to_all | solution.py:27
  223.4 84.6 %all-gather.3.cloned.1.call-start = ((), (), s32[]{:S(2)}) async-start(), calls=%async_computation.8 | async-start | bytes 1114112 | tf_op jit(solution)/shard_map/all_gather | solution.py:84
  225.4 86.0 %copy-start.5 = (bf16[512,512]{1,0:T(8,128)(2,1)S(1)}, bf16[512,512]{1,0:T(8,128)(2,1)}, u32[]{:S(2)}) copy-start(bf16[512,512]{1,0:T(8,128)(2,1)} %param.8) | copy-start | bytes 1572868
  239.1 73.7 %all-to-all-start.7 = ((bf16[16,32,512]{2,1,0:T(8,128)(2,1)}), bf16[16,32,512]{2,1,0:T(8,128)(2,1)S(1)}, u32[]{:S(2)}, u32[]{:S(2)}) async-start(bf16[16,32,512]{2,1,0:T(8,128)(2,1)} %broadcast_in_dim.16), calls=%async_computation.7 | async-start | bytes 1048576 | tf_op jit(solution)/shard_map/all_to_all | solution.py:27
Sparse Core Ops, SparseCore 0:
  226.9 81.0 all-gather.2

commit v2 on v1

v2 whole, which is shorter than its diff:
```python
import math

import jax
import jax.numpy as jnp
from jax import lax
from jax.sharding import Mesh, PartitionSpec as P

DP = ("zl", "x")
CTX = ("zh", "y", "c")
YC = ("y", "c")
BF = jnp.bfloat16
F32 = jnp.float32


def mm(a, b):
    return jnp.dot(a, b, preferred_element_type=F32)


def mm_t(a, b):
    return lax.dot_general(a, b, (((1,), (1,)), ((), ())), preferred_element_type=F32)


def mm_tl(a, b):
    return lax.dot_general(a, b, (((0,), (0,)), ((), ())), preferred_element_type=F32)


def swap(blocks, axes):
    return lax.all_to_all(blocks, axes, 0, 0, tiled=True)


def shift(block, axis, step):
    n = lax.axis_size(axis)
    return lax.ppermute(block, axis, [(i, (i + step) % n) for i in range(n)])


def exchange(blocks, axis, order):
    n = len(blocks)
    got = [blocks[0]] + [None] * (n - 1)
    for m in order:
        got[(n - m) % n] = shift(blocks[m], axis, m)
    return got


def pick(stack, first, n):
    return [lax.dynamic_index_in_dim(stack, (first + m) % n, 0, keepdims=False) for m in range(n)]


def per_device(tokens, cotangent, gate_weight, out_weight, left_matrix, right_factor):
    x = tokens[0]
    cot = cotangent[0]
    left = left_matrix[0]
    tok, ch = x.shape
    pos, nb, _ = right_factor.shape
    seqs = lax.axis_size(DP)
    ctx = lax.axis_size(CTX)
    nz, ny, nx = (lax.axis_size(a) for a in ("zh", "y", "x"))
    yi, ci, xi = (lax.axis_index(a) for a in ("y", "c", "x"))
    weight_scale = 1.0 / math.sqrt(seqs * ctx * tok)
    factor_scale = 1.0 / math.sqrt(seqs * ch)

    first_mix = mm(left, x).astype(BF)
    first_moved = swap(first_mix.reshape(nb, pos, ch), CTX)

    gate_pre = mm(x, gate_weight)
    grad_hidden = mm_t(cot, out_weight)
    sig = jax.nn.sigmoid(gate_pre)
    activated = gate_pre * sig
    slope = sig * (1.0 + gate_pre * (1.0 - sig))
    grad_second = (grad_hidden * activated).astype(BF)

    same = jnp.eye(pos, dtype=BF)
    wide = (right_factor.transpose(1, 0, 2)[:, :, :, None] * same[None, :, None, :]).reshape(nb * pos, nb * pos)

    second_moved = mm(wide, first_moved.reshape(nb * pos, ch)).astype(BF)
    both = jnp.concatenate([second_moved.reshape(nb, pos, ch), grad_second.reshape(nb, pos, ch)], 1)
    both = swap(both, CTX)
    second_mix = both[:, :pos].reshape(tok, ch)
    grad_moved = both[:, pos:]

    first_grad_moved = mm_tl(wide, grad_moved.reshape(nb * pos, ch)).astype(BF)
    initial_gradient = swap(first_grad_moved.reshape(nb, pos, ch), CTX).reshape(tok, ch)

    mixed = second_mix.astype(F32)
    hidden = (mixed * activated).astype(BF)
    grad_gate_pre = (grad_hidden * mixed * slope).astype(BF)
    term_gate = mm_tl(x, grad_gate_pre).astype(BF)
    term_out = mm_tl(hidden, cot).astype(BF)

    share = ch // ctx
    terms = jnp.stack([term_gate, term_out]).reshape(2, nz, ny, 2, share, ch)
    mine = lax.dynamic_index_in_dim(terms, ci, 3, keepdims=False)
    other = lax.dynamic_index_in_dim(terms, 1 - ci, 3, keepdims=False)
    terms = (mine.astype(F32) + shift(other, "c", 1).astype(F32)).astype(BF)
    terms = pick(jnp.moveaxis(terms, 2, 0), yi, ny)
    terms = sum(b.astype(F32) for b in exchange(terms, "y", (2, 1, 3))).astype(BF)
    terms = jnp.moveaxis(terms, 1, 0).reshape(nz, 2 * share, ch)
    terms = swap(terms, "zh").astype(F32).sum(0).astype(BF)

    term_right = jnp.einsum("kpd,jpd->pkj", grad_moved, first_moved, preferred_element_type=F32)
    term_right = term_right.reshape(-1, ch).astype(BF)

    result = mm(hidden, out_weight).astype(BF)
    through_gate = mm_t(grad_gate_pre, gate_weight)

    term_left = mm_t(initial_gradient, x).astype(BF)
    part = pick(term_left.reshape(nx, tok // nx, tok), xi, nx)
    part = sum(b.astype(F32) for b in exchange(part, "x", (2, 1, 3))).astype(BF)

    small = jnp.concatenate([part, terms, term_right], 0)
    small = lax.all_gather(small, "zl", axis=0).astype(F32).sum(0).astype(BF)
    small = swap(jnp.broadcast_to(small[None], (nx,) + small.shape), "x")
    sum_left = small[:, : tok // nx].reshape(1, tok, tok).astype(F32)
    small = small[:, tok // nx :].astype(F32).sum(0)
    sum_gate = small[:share]
    sum_out = small[share : 2 * share]
    sum_right = small[2 * share :].reshape(pos, nb, nb)

    grad_tokens = (mm_tl(left, initial_gradient) + through_gate).astype(BF)

    return (
        result[None],
        grad_tokens[None],
        sum_gate * weight_scale,
        sum_out * weight_scale,
        sum_left * factor_scale,
        sum_right * factor_scale,
    )


def solution(mesh):
    fine = Mesh(mesh.devices.reshape(4, 4, 4, 4, 2), DP + CTX)
    tok = P(DP, CTX, None)
    own = P(CTX, None, None)
    return jax.shard_map(
        per_device,
        mesh=fine,
        in_specs=(tok, tok, P(), P(), own, own),
        out_specs=(tok, tok, P(CTX, None), P(CTX, None), own, own),
        check_vma=False,
    )
```

time: 322 us -> 223 us (0.69)
  the two profiles are of different devices: /device:TPU:8 before, /device:TPU:2 now
where the time goes in v2:
time: 223 us; the launch traced here: 221 us
  waiting for transfers between devices  77.5 us (35%)
  starting transfers between devices  77 us (35%)
  blocking collectives  17.6 us (8%)
  local copies, waits for them, and re-layouts  16.7 us (7%)
  matrix products  16.6 us (7%)
  other arithmetic  15 us (7%)
    all_to_all x5, waiting for transfers between devices, swap(): return lax.all_to_all(blocks, axes, 0, 0, tiled=True)  68.8 us
    all_to_all x5, starting transfers between devices, swap(): return lax.all_to_all(blocks, axes, 0, 0, tiled=True)  53.1 us
    ppermute x7, starting transfers between devices, shift(): return lax.ppermute(block, axis, [(i, (i + step) % n) for i in range(n)])  23.8 us
    all_gather x1, blocking collectives, per_device(): small = lax.all_gather(small, 'zl', axis=0).astype(F32).sum(0).astype(BF)  17.6 us
    ppermute x7, waiting for transfers between devices, shift(): return lax.ppermute(block, axis, [(i, (i + step) % n) for i in range(n)])  8.69 us
    mul x1, local copies, waits for them, and re-layouts, per_device(): right_factor.transpose(1, 0, 2)[:, :, :, None] * same[None, :, None, :]  7.77 us
    dot_general x4, matrix products, mm(): return jnp.dot(a, b, preferred_element_type=F32)  5.41 us
    dot_general x3, matrix products, mm_t(): lax.dot_general(a, b, (((1,), (1,)), ((), ())), preferred_element_type=F32)  4.79 us
  transfers between devices with their start and end apart: 12, of which 8 were waited for; matrix products, arithmetic and copies ran while one was open for 16% of the time, Pallas kernels for 0%

profile of v2, /device:TPU:2, one launch (start us, length us, event | category | flops | bytes accessed | tf_op | source)
XLA Modules:
  0.0 221.5 jit_solution(4585352617090983586)
XLA Ops:
  1.7 2.3 %convolution_convert_fusion.6 = bf16[512,512]{1,0:T(8,128)(2,1)} fusion(bf16[1,512,512]{2,1,0:T(8,128)(2,1)S(1)} %copy-done, bf16[1,512,512]{2,1,0:T(8,128)(2,1)} %param.10), kind=kOutput, calls=%fused_computation.11 | convolution fusion | flops 268697600 | bytes 1572864 | tf_op jit(solution)/shard_map/dot_general | solution.py:16
  4.0 18.1 %all-to-all-start = ((bf16[32,16,512]{2,1,0:T(8,128)(2,1)}), bf16[32,16,512]{2,1,0:T(8,128)(2,1)S(1)}, u32[]{:S(2)}, u32[]{:S(2)}) async-start(bf16[32,16,512]{2,1,0:T(8,128)(2,1)} %bitcast.3), calls=%async_computation | async-start | bytes 1048576 | tf_op jit(solution)/shard_map/all_to_all | solution.py:28
  23.1 3.9 %broadcast_multiply_fusion = bf16[32,16,32,16]{3,2,1,0:T(8,128)(2,1)} fusion(bf16[16,16]{1,0:T(8,128)(2,1)S(1)} %fusion.28, bf16[32,16,32]{2,1,0:T(8,128)(2,1)S(1)} %copy.30), kind=kLoop, calls=%fused_computation | loop fusion | flops 262144 | bytes 557568 | tf_op jit(solution)/shard_map/mul | solution.py:72
  26.9 7.8 %mul.83 = bf16[512,512]{1,0:T(8,128)(2,1)S(1)} reshape(bf16[32,16,32,16]{3,2,1,0:T(8,128)(2,1)} %broadcast_multiply_fusion) | data formatting | bytes 1048576 | tf_op jit(solution)/shard_map/mul | solution.py:72
  35.2 2.8 %multiply_convert_fusion = (bf16[512,512]{1,0:T(8,128)(2,1)}, f32[512,512]{1,0:T(8,128)}) fusion(f32[512,512]{1,0:T(8,128)S(1)} %fusion.16, bf16[512,512]{1,0:T(8,128)(2,1)} %param.9, bf16[1,512,512]{2,1,0:T(8,128)(2,1)} %param.7), kind=kOutput, calls=%fused_computation.27 | convolution fusion | flops 270008320 | bytes 3670016 | tf_op jit(solution)/shard_map/dot_general | solution.py:20
  38.0 13.3 %all-to-all-done = bf16[32,16,512]{2,1,0:T(8,128)(2,1)S(1)} async-done(((bf16[32,16,512]{2,1,0:T(8,128)(2,1)}), bf16[32,16,512]{2,1,0:T(8,128)(2,1)S(1)}, u32[]{:S(2)}, u32[]{:S(2)}) %all-to-all-start) | async-done | bytes 524320 | tf_op jit(solution)/shard_map/all_to_all | solution.py:28
  51.8 2.1 pad_maximum_fusion
  53.9 9.0 %all-to-all-start.1 = ((bf16[32,32,512]{2,1,0:T(8,128)(2,1)}), bf16[32,32,512]{2,1,0:T(8,128)(2,1)S(1)}, u32[]{:S(2)}, u32[]{:S(2)}) async-start(bf16[32,32,512]{2,1,0:T(8,128)(2,1)} %pad_maximum_fusion), calls=%async_computation.1 | async-start | bytes 2097152 | tf_op jit(solution)/shard_map/all_to_all | solution.py:28
  62.9 52.3 %all-to-all-done.1 = bf16[32,32,512]{2,1,0:T(8,128)(2,1)S(1)} async-done(((bf16[32,32,512]{2,1,0:T(8,128)(2,1)}), bf16[32,32,512]{2,1,0:T(8,128)(2,1)S(1)}, u32[]{:S(2)}, u32[]{:S(2)}) %all-to-all-start.1) | async-done | bytes 1048608 | tf_op jit(solution)/shard_map/all_to_all | solution.py:28
  117.3 8.5 %all-to-all-start.2 = ((bf16[32,16,512]{2,1,0:T(8,128)(2,1)}), bf16[32,16,512]{2,1,0:T(8,128)(2,1)S(1)}, u32[]{:S(2)}, u32[]{:S(2)}) async-start(bf16[32,16,512]{2,1,0:T(8,128)(2,1)} %bitcast.11), calls=%async_computation.2 | async-start | bytes 1048576 | tf_op jit(solution)/shard_map/all_to_all | solution.py:28
  125.8 1.9 fusion.5
  128.2 1.5 convolution_convert_fusion
  131.5 2.2 collective-permute-start.3
  133.7 1.8 collective-permute-done.3
  138.4 4.9 %collective-permute-start.4 = (bf16[2,4,16,512]{3,2,0,1:T(8,128)(2,1)}, bf16[2,4,16,512]{3,2,0,1:T(8,128)(2,1)S(1)}, u32[]{:S(2)}, u32[]{:S(2)}) collective-permute-start(bf16[2,4,16,512]{3,2,0,1:T(8,128)(2,1)} %get-tuple-element.33), channel_id=1, source_target_pairs={{0,6},{2,0},{4,2},{6,4},{1,7},{3,1},{5,3},{7,5},{8,14},{10,8},{12,... | collective-permute-start | bytes 393224 | tf_op jit(solution)/shard_map/ppermute | solution.py:33
  143.3 2.8 %collective-permute-start.5 = (bf16[2,4,16,512]{3,2,0,1:T(8,128)(2,1)S(1)}, bf16[2,4,16,512]{3,2,0,1:T(8,128)(2,1)}, u32[]{:S(2)}, u32[]{:S(2)}) collective-permute-start(bf16[2,4,16,512]{3,2,0,1:T(8,128)(2,1)S(1)} %get-tuple-element.35), channel_id=1, source_target_pairs={{0,4},{2,6},{4,0},{6,2},{1,5},{3,7},{5,1},{7,3},{8,12},{10,14},{12... | collective-permute-start | bytes 393224 | tf_op jit(solution)/shard_map/ppermute | solution.py:33
  146.1 2.8 %collective-permute-start.6 = (bf16[2,4,16,512]{3,2,0,1:T(8,128)(2,1)S(1)}, bf16[2,4,16,512]{3,2,0,1:T(8,128)(2,1)}, u32[]{:S(2)}, u32[]{:S(2)}) collective-permute-start(bf16[2,4,16,512]{3,2,0,1:T(8,128)(2,1)S(1)} %get-tuple-element.34), channel_id=1, source_target_pairs={{0,2},{2,4},{4,6},{6,0},{1,3},{3,5},{5,7},{7,1},{8,10},{10,12},{12... | collective-permute-start | bytes 393224 | tf_op jit(solution)/shard_map/ppermute | solution.py:33
  148.9 1.6 collective-permute-done.4
  150.5 3.0 %collective-permute-done.5 = bf16[2,4,16,512]{3,2,0,1:T(8,128)(2,1)} collective-permute-done((bf16[2,4,16,512]{3,2,0,1:T(8,128)(2,1)S(1)}, bf16[2,4,16,512]{3,2,0,1:T(8,128)(2,1)}, u32[]{:S(2)}, u32[]{:S(2)}) %collective-permute-start.5) | collective-permute-done | bytes 131104 | tf_op jit(solution)/shard_map/ppermute | solution.py:33
  153.5 2.3 %collective-permute-done.6 = bf16[2,4,16,512]{3,2,0,1:T(8,128)(2,1)} collective-permute-done((bf16[2,4,16,512]{3,2,0,1:T(8,128)(2,1)S(1)}, bf16[2,4,16,512]{3,2,0,1:T(8,128)(2,1)}, u32[]{:S(2)}, u32[]{:S(2)}) %collective-permute-start.6) | collective-permute-done | bytes 131104 | tf_op jit(solution)/shard_map/ppermute | solution.py:33
  155.8 1.7 fusion.24
  157.5 11.0 %all-to-all-start.3 = ((bf16[4,32,512]{2,1,0:T(8,128)(2,1)}), bf16[4,32,512]{2,1,0:T(8,128)(2,1)S(1)}, u32[]{:S(2)}, u32[]{:S(2)}) async-start(bf16[4,32,512]{2,1,0:T(8,128)(2,1)} %bitcast.32), calls=%async_computation.3 | async-start | bytes 262144 | tf_op jit(solution)/shard_map/all_to_all | solution.py:28
  169.7 3.2 %collective-permute-start = (bf16[128,512]{1,0:T(8,128)(2,1)}, bf16[128,512]{1,0:T(8,128)(2,1)}, u32[]{:S(2)}, u32[]{:S(2)}) collective-permute-start(bf16[128,512]{1,0:T(8,128)(2,1)} %get-tuple-element.30), channel_id=1, source_target_pairs={{0,96},{32,0},{64,32},{96,64},{1,97},{33,1},{65,33},{97,65},{2,98}... | collective-permute-start | bytes 393224 | tf_op jit(solution)/shard_map/ppermute | solution.py:33
  172.9 4.0 %collective-permute-start.1 = (bf16[128,512]{1,0:T(8,128)(2,1)}, bf16[128,512]{1,0:T(8,128)(2,1)}, u32[]{:S(2)}, u32[]{:S(2)}) collective-permute-start(bf16[128,512]{1,0:T(8,128)(2,1)} %get-tuple-element.32), channel_id=1, source_target_pairs={{0,64},{32,96},{64,0},{96,32},{1,65},{33,97},{65,1},{97,33},{2,66}... | collective-permute-start | bytes 393224 | tf_op jit(solution)/shard_map/ppermute | solution.py:33
  176.9 4.0 %collective-permute-start.2 = (bf16[128,512]{1,0:T(8,128)(2,1)S(1)}, bf16[128,512]{1,0:T(8,128)(2,1)}, u32[]{:S(2)}, u32[]{:S(2)}) collective-permute-start(bf16[128,512]{1,0:T(8,128)(2,1)S(1)} %get-tuple-element.31), channel_id=1, source_target_pairs={{0,32},{32,64},{64,96},{96,0},{1,33},{33,65},{65,97},{97,1},{2,34}... | collective-permute-start | bytes 393224 | tf_op jit(solution)/shard_map/ppermute | solution.py:33
  181.0 1.7 convolution_convert_fusion.7
  185.2 17.6 %all-gather = bf16[768,512]{1,0:T(8,128)(2,1)S(1)} all-gather(bf16[192,512]{1,0:T(8,128)(2,1)S(1)} %pad_maximum_fusion.1), channel_id=2, replica_groups=mesh['zl'=4,'x'=4,'zh'=4,'y'=4,'c'=2] {'zl'}, dimensions={0}, use_global_device_ids=true | all-gather | bytes 983040 | tf_op jit(solution)/shard_map/all_gather | solution.py:110
  203.9 6.6 %all-to-all-start.4 = ((bf16[4,192,512]{2,1,0:T(8,128)(2,1)}), bf16[4,192,512]{2,1,0:T(8,128)(2,1)S(1)}, u32[]{:S(2)}, u32[]{:S(2)}) async-start(bf16[4,192,512]{2,1,0:T(8,128)(2,1)} %broadcast_in_dim.16), calls=%async_computation.4 | async-start | bytes 1572864 | tf_op jit(solution)/shard_map/all_to_all | solution.py:28
  210.5 2.3 %fusion.2 = bf16[1,512,512]{2,1,0:T(8,128)(2,1)} fusion(bf16[512,512]{1,0:T(8,128)(2,1)S(1)} %get-tuple-element.25, bf16[512,512]{1,0:T(8,128)(2,1)} %param.9), kind=kOutput, calls=%fused_computation.14 | convolution fusion | flops 268697600 | bytes 1572864 | tf_op jit(solution)/shard_map/dot_general | solution.py:16
  212.8 1.5 convolution_bitcast_fusion
  214.3 1.5 fusion.1
  216.8 2.1 all-to-all-done.4
  (42 shorter events, 18.5 us)
Async XLA Ops:
  0.6 1.0 copy-start
  4.0 47.4 %all-to-all-start = ((bf16[32,16,512]{2,1,0:T(8,128)(2,1)}), bf16[32,16,512]{2,1,0:T(8,128)(2,1)S(1)}, u32[]{:S(2)}, u32[]{:S(2)}) async-start(bf16[32,16,512]{2,1,0:T(8,128)(2,1)} %bitcast.3), calls=%async_computation | async-start | bytes 1048576 | tf_op jit(solution)/shard_map/all_to_all | solution.py:28
  23.0 11.7 %copy-start.3 = (bf16[512,512]{1,0:T(8,128)(2,1)S(1)}, bf16[512,512]{1,0:T(8,128)(2,1)}, u32[]{:S(2)}) copy-start(bf16[512,512]{1,0:T(8,128)(2,1)} %param.8) | copy-start | bytes 1572868
  51.3 2.6 %copy-start.1 = (bf16[32,16,512]{2,1,0:T(8,128)(2,1)}, bf16[32,16,512]{2,1,0:T(8,128)(2,1)S(1)}, u32[]{:S(2)}) copy-start(bf16[32,16,512]{2,1,0:T(8,128)(2,1)S(1)} %all-to-all-done) | copy-start | bytes 1572868
  53.9 61.3 %all-to-all-start.1 = ((bf16[32,32,512]{2,1,0:T(8,128)(2,1)}), bf16[32,32,512]{2,1,0:T(8,128)(2,1)S(1)}, u32[]{:S(2)}, u32[]{:S(2)}) async-start(bf16[32,32,512]{2,1,0:T(8,128)(2,1)} %pad_maximum_fusion), calls=%async_computation.1 | async-start | bytes 2097152 | tf_op jit(solution)/shard_map/all_to_all | solution.py:28
  116.0 1.3 copy-start.5
  117.3 40.2 %all-to-all-start.2 = ((bf16[32,16,512]{2,1,0:T(8,128)(2,1)}), bf16[32,16,512]{2,1,0:T(8,128)(2,1)S(1)}, u32[]{:S(2)}, u32[]{:S(2)}) async-start(bf16[32,16,512]{2,1,0:T(8,128)(2,1)} %bitcast.11), calls=%async_computation.2 | async-start | bytes 1048576 | tf_op jit(solution)/shard_map/all_to_all | solution.py:28
  129.8 51.2 %copy-start.2 = (bf16[32,16,512]{2,1,0:T(8,128)(2,1)S(1)}, bf16[32,16,512]{2,1,0:T(8,128)(2,1)}, u32[]{:S(2)}) copy-start(bf16[32,16,512]{2,1,0:T(8,128)(2,1)} %copy-done.1) | copy-start | bytes 1572868
  131.5 4.0 %collective-permute-start.3 = (bf16[2,4,4,16,512]{4,3,0,1,2:T(8,128)(2,1)}, bf16[2,4,4,16,512]{4,3,0,1,2:T(8,128)(2,1)S(1)}, u32[]{:S(2)}, u32[]{:S(2)}) collective-permute-start(bf16[2,4,4,16,512]{4,3,0,1,2:T(8,128)(2,1)} %bitcast.90), channel_id=1, source_target_pairs={{0,1},{1,0},{2,3},{3,2},{4,5},{5,4},{6,7},{7,6},{8,9},{9,8},{10,11... | collective-permute-start | bytes 1572872 | tf_op jit(solution)/shard_map/ppermute | solution.py:33
  135.5 0.8 copy-start.4
  138.4 12.1 %collective-permute-start.4 = (bf16[2,4,16,512]{3,2,0,1:T(8,128)(2,1)}, bf16[2,4,16,512]{3,2,0,1:T(8,128)(2,1)S(1)}, u32[]{:S(2)}, u32[]{:S(2)}) collective-permute-start(bf16[2,4,16,512]{3,2,0,1:T(8,128)(2,1)} %get-tuple-element.33), channel_id=1, source_target_pairs={{0,6},{2,0},{4,2},{6,4},{1,7},{3,1},{5,3},{7,5},{8,14},{10,8},{12,... | collective-permute-start | bytes 393224 | tf_op jit(solution)/shard_map/ppermute | solution.py:33
  143.3 10.2 %collective-permute-start.5 = (bf16[2,4,16,512]{3,2,0,1:T(8,128)(2,1)S(1)}, bf16[2,4,16,512]{3,2,0,1:T(8,128)(2,1)}, u32[]{:S(2)}, u32[]{:S(2)}) collective-permute-start(bf16[2,4,16,512]{3,2,0,1:T(8,128)(2,1)S(1)} %get-tuple-element.35), channel_id=1, source_target_pairs={{0,4},{2,6},{4,0},{6,2},{1,5},{3,7},{5,1},{7,3},{8,12},{10,14},{12... | collective-permute-start | bytes 393224 | tf_op jit(solution)/shard_map/ppermute | solution.py:33
  146.1 9.8 %collective-permute-start.6 = (bf16[2,4,16,512]{3,2,0,1:T(8,128)(2,1)S(1)}, bf16[2,4,16,512]{3,2,0,1:T(8,128)(2,1)}, u32[]{:S(2)}, u32[]{:S(2)}) collective-permute-start(bf16[2,4,16,512]{3,2,0,1:T(8,128)(2,1)S(1)} %get-tuple-element.34), channel_id=1, source_target_pairs={{0,2},{2,4},{4,6},{6,0},{1,3},{3,5},{5,7},{7,1},{8,10},{10,12},{12... | collective-permute-start | bytes 393224 | tf_op jit(solution)/shard_map/ppermute | solution.py:33
  157.5 26.5 %all-to-all-start.3 = ((bf16[4,32,512]{2,1,0:T(8,128)(2,1)}), bf16[4,32,512]{2,1,0:T(8,128)(2,1)S(1)}, u32[]{:S(2)}, u32[]{:S(2)}) async-start(bf16[4,32,512]{2,1,0:T(8,128)(2,1)} %bitcast.32), calls=%async_computation.3 | async-start | bytes 262144 | tf_op jit(solution)/shard_map/all_to_all | solution.py:28
  169.7 14.3 %collective-permute-start = (bf16[128,512]{1,0:T(8,128)(2,1)}, bf16[128,512]{1,0:T(8,128)(2,1)}, u32[]{:S(2)}, u32[]{:S(2)}) collective-permute-start(bf16[128,512]{1,0:T(8,128)(2,1)} %get-tuple-element.30), channel_id=1, source_target_pairs={{0,96},{32,0},{64,32},{96,64},{1,97},{33,1},{65,33},{97,65},{2,98}... | collective-permute-start | bytes 393224 | tf_op jit(solution)/shard_map/ppermute | solution.py:33
  172.9 11.2 %collective-permute-start.1 = (bf16[128,512]{1,0:T(8,128)(2,1)}, bf16[128,512]{1,0:T(8,128)(2,1)}, u32[]{:S(2)}, u32[]{:S(2)}) collective-permute-start(bf16[128,512]{1,0:T(8,128)(2,1)} %get-tuple-element.32), channel_id=1, source_target_pairs={{0,64},{32,96},{64,0},{96,32},{1,65},{33,97},{65,1},{97,33},{2,66}... | collective-permute-start | bytes 393224 | tf_op jit(solution)/shard_map/ppermute | solution.py:33
  176.9 7.1 %collective-permute-start.2 = (bf16[128,512]{1,0:T(8,128)(2,1)S(1)}, bf16[128,512]{1,0:T(8,128)(2,1)}, u32[]{:S(2)}, u32[]{:S(2)}) collective-permute-start(bf16[128,512]{1,0:T(8,128)(2,1)S(1)} %get-tuple-element.31), channel_id=1, source_target_pairs={{0,32},{32,64},{64,96},{96,0},{1,33},{33,65},{65,97},{97,1},{2,34}... | collective-permute-start | bytes 393224 | tf_op jit(solution)/shard_map/ppermute | solution.py:33
  203.9 14.9 %all-to-all-start.4 = ((bf16[4,192,512]{2,1,0:T(8,128)(2,1)}), bf16[4,192,512]{2,1,0:T(8,128)(2,1)S(1)}, u32[]{:S(2)}, u32[]{:S(2)}) async-start(bf16[4,192,512]{2,1,0:T(8,128)(2,1)} %broadcast_in_dim.16), calls=%async_computation.4 | async-start | bytes 1572864 | tf_op jit(solution)/shard_map/all_to_all | solution.py:28

commit v3 on v2

v3 whole, which is shorter than its diff:
```python
import functools
import math

import jax
import jax.numpy as jnp
from jax import lax
from jax.experimental import pallas as pl
from jax.experimental.pallas import tpu as pltpu
from jax.sharding import Mesh, PartitionSpec as P

DP = ("zl", "x")
CTX = ("zh", "y", "c")
YC = ("y", "c")
BF = jnp.bfloat16
F32 = jnp.float32


def mm(a, b):
    return jnp.dot(a, b, preferred_element_type=F32)


def mm_t(a, b):
    return lax.dot_general(a, b, (((1,), (1,)), ((), ())), preferred_element_type=F32)


def mm_tl(a, b):
    return lax.dot_general(a, b, (((0,), (0,)), ((), ())), preferred_element_type=F32)


def swap(blocks, axes):
    return lax.all_to_all(blocks, axes, 0, 0, tiled=True)


def shift(block, axis, step):
    n = lax.axis_size(axis)
    return lax.ppermute(block, axis, [(i, (i + step) % n) for i in range(n)])


def exchange(blocks, axis, order):
    n = len(blocks)
    got = [blocks[0]] + [None] * (n - 1)
    for m in order:
        got[(n - m) % n] = shift(blocks[m], axis, m)
    return got


def pick(stack, first, n):
    return [lax.dynamic_index_in_dim(stack, (first + m) % n, 0, keepdims=False) for m in range(n)]


LIMIT = pltpu.CompilerParams(vmem_limit_bytes=56 * 2**20)


def in_vmem(body, out_shape, *args):
    vmem = pl.BlockSpec(memory_space=pltpu.VMEM)
    return pl.pallas_call(
        body,
        out_shape=out_shape,
        in_specs=[vmem] * len(args),
        out_specs=jax.tree.map(lambda _: vmem, out_shape),
        compiler_params=pltpu.CompilerParams(vmem_limit_bytes=32 * 2**20),
    )(*args)


def from_hbm(body, out_shape, *args):
    n = len(args)

    def whole(*refs):
        here, out, there, sems = refs[:n], refs[n:-n - 1], refs[-n - 1 : -1], refs[-1]
        copies = [pltpu.make_async_copy(h, t, sems.at[i]) for i, (h, t) in enumerate(zip(here, there))]
        for copy in copies:
            copy.start()
        body(lambda *which: [copies[i].wait() for i in which], *there, *out)

    return pl.pallas_call(
        whole,
        out_shape=out_shape,
        in_specs=[pl.BlockSpec(memory_space=pltpu.HBM)] * n,
        out_specs=jax.tree.map(lambda _: pl.BlockSpec(memory_space=pltpu.VMEM), out_shape),
        scratch_shapes=[pltpu.VMEM(a.shape, a.dtype) for a in args] + [pltpu.SemaphoreType.DMA((n,))],
        compiler_params=LIMIT,
    )(*args)


def front_body(ready, left, x, gate_weight, cot, out_weight, both):
    nb, two, ch = both.shape
    pos = two // 2
    ready(0, 1)
    both[:, :pos] = mm(left[...], x[...]).astype(BF).reshape(nb, pos, ch)
    ready(2, 3, 4)
    gate_pre = mm(x[...], gate_weight[...])
    grad_hidden = mm_t(cot[...], out_weight[...])
    activated = gate_pre * jax.nn.sigmoid(gate_pre)
    both[:, pos:] = (grad_hidden * activated).astype(BF).reshape(nb, pos, ch)


def middle_body(moved, wide, wide_t, both, right):
    nb, two, ch = both.shape
    pos = two // 2
    rows = nb * pos
    first = moved[:, :pos].reshape(rows, ch)
    grad = moved[:, pos:].reshape(rows, ch)
    both[:, :pos] = mm(wide[...], first).astype(BF).reshape(nb, pos, ch)
    both[:, pos:] = mm(wide_t[...], grad).astype(BF).reshape(nb, pos, ch)
    place = lax.broadcasted_iota(jnp.int32, (rows, rows), 0) % pos
    other = lax.broadcasted_iota(jnp.int32, (rows, rows), 1) % pos
    kept = jnp.where(place == other, mm_t(grad, first), 0.0).astype(BF)
    column = lax.broadcasted_iota(jnp.int32, (rows, 128), 0) // pos
    choose = (column == lax.broadcasted_iota(jnp.int32, (rows, 128), 1)).astype(BF)
    right[...] = mm(kept, choose).astype(BF)


def gate_body(ready, back, activated, sloped, x, cot, hidden, grad_gate_pre, terms):
    tok, ch = x.shape
    yc, nl, nz, part, _ = terms.shape
    pos = back.shape[1] // 2
    ready(0, 1, 2)
    mixed = back[:, :pos].reshape(tok, ch).astype(F32)
    grad_gate_pre[...] = (mixed * sloped[...]).astype(BF)
    hidden[...] = (mixed * activated[...]).astype(BF)
    ready(3, 4)
    for i, term in enumerate((mm_tl(x[...], grad_gate_pre[...]), mm_tl(hidden[...], cot[...]))):
        term = term.reshape(nz, yc, nl // 2, part, ch)
        for half in range(nl // 2):
            for z in range(nz):
                terms[:, i * (nl // 2) + half, z] = term[z, :, half].astype(BF)


def sum_body(parts, total):
    total[...] = parts[...].astype(F32).sum(0).astype(BF)


def pack_body(near, one, two, three, terms, packed):
    part = near[...].astype(F32) + one[...].astype(F32) + two[...].astype(F32) + three[...].astype(F32)
    term = terms[...].astype(F32).sum(0)
    row = jnp.concatenate([part, term], 0).astype(BF)
    packed[...] = jnp.broadcast_to(row[None], packed.shape)


def finish_body(weight_scale, factor_scale, packed, left, gate, out, right):
    seqs, rows, ch = packed.shape
    size = left.shape[0] // seqs
    left[...] = packed[:, :size].astype(F32).reshape(left.shape) * factor_scale
    rest = packed[:, size:].astype(F32)
    right[...] = rest[:, :8, :128] * factor_scale
    share = gate.shape[0]
    terms = rest[:, 8:].reshape(-1, 4, 8, ch).sum(1).reshape(2 * share, ch) * weight_scale
    gate[...] = terms[:share]
    out[...] = terms[share:]


def per_device(tokens, cotangent, gate_weight, out_weight, left_matrix, right_factor):
    x = tokens[0]
    cot = cotangent[0]
    left = left_matrix[0]
    tok, ch = x.shape
    pos, nb, _ = right_factor.shape
    seqs = lax.axis_size(DP)
    ctx = lax.axis_size(CTX)
    nz, nl, nx = (lax.axis_size(a) for a in ("zh", "zl", "x"))
    li, xi = lax.axis_index("zl"), lax.axis_index("x")
    weight_scale = 1.0 / math.sqrt(seqs * ctx * tok)
    factor_scale = 1.0 / math.sqrt(seqs * ch)

    pair = jax.ShapeDtypeStruct((nb, 2 * pos, ch), BF)
    sent = from_hbm(front_body, pair, left, x, gate_weight, cot, out_weight)
    moved = swap(sent, CTX)

    gate_pre = mm(x, gate_weight)
    grad_hidden = mm_t(cot, out_weight)
    sig = jax.nn.sigmoid(gate_pre)
    activated = gate_pre * sig
    slope = sig * (1.0 + gate_pre * (1.0 - sig))

    same = jnp.eye(pos, dtype=BF)[None, :, None, :]
    wide = (right_factor.transpose(1, 0, 2)[:, :, :, None] * same).reshape(nb * pos, nb * pos)
    wide_t = (right_factor.transpose(2, 0, 1)[:, :, :, None] * same).reshape(nb * pos, nb * pos)
    right_shape = jax.ShapeDtypeStruct((nb * pos, 128), BF)
    sent, term_right = in_vmem(middle_body, (pair, right_shape), moved, wide, wide_t)
    back = swap(sent, CTX)

    term_right = term_right[:, :nb].reshape(nb, pos, nb).transpose(1, 0, 2).reshape(nl, nx, -1, 128)
    term_right = jnp.pad(term_right, ((0, 0), (0, 0), (0, 0), (0, ch - 128)))

    share = ch // ctx
    yc = lax.axis_size(YC)
    token_pair = jax.ShapeDtypeStruct((tok, ch), BF)
    gated = (token_pair, token_pair, jax.ShapeDtypeStruct((yc, nl, nz, 2 * share // nl, ch), BF))
    hidden, grad_gate_pre, terms = from_hbm(gate_body, gated, back, activated, grad_hidden * slope, x, cot)
    initial_gradient = back[:, pos:].reshape(tok, ch)

    terms = swap(terms.reshape(yc, nz * 2 * share, ch), YC)
    terms = in_vmem(sum_body, jax.ShapeDtypeStruct(terms.shape[1:], BF), terms)
    terms = swap(terms.reshape(nl * nz, -1, ch), ("zl", "zh"))

    result = mm(hidden, out_weight).astype(BF)
    through_gate = mm_t(grad_gate_pre, gate_weight)

    term_left = mm_t(initial_gradient, x).astype(BF)
    part = jnp.concatenate([term_left.reshape(nl, nx, -1, tok), term_right], 2)
    part = jnp.moveaxis(part, 1, 0)
    part = sum(b.astype(F32) for b in exchange(pick(part, xi, nx), "x", (2, 1, 3))).astype(BF)
    near, one, two, three = exchange(pick(part, li, nl), "zl", (2, 1, 3))
    packed = jax.ShapeDtypeStruct((seqs, near.shape[0] + terms.shape[1], ch), BF)
    packed = swap(in_vmem(pack_body, packed, near, one, two, three, terms), DP)
    finished = (
        jax.ShapeDtypeStruct((tok, tok), F32),
        jax.ShapeDtypeStruct((share, ch), F32),
        jax.ShapeDtypeStruct((share, ch), F32),
        jax.ShapeDtypeStruct((seqs, 8, 128), F32),
    )
    finish = functools.partial(finish_body, weight_scale, factor_scale)
    sum_left, sum_gate, sum_out, sum_right = in_vmem(finish, finished, packed)

    grad_tokens = (mm_tl(left, initial_gradient) + through_gate).astype(BF)

    return (
        result[None],
        grad_tokens[None],
        sum_gate,
        sum_out,
        sum_left[None],
        sum_right.reshape(pos, nb, nb),
    )


def solution(mesh):
    fine = Mesh(mesh.devices.reshape(4, 4, 4, 4, 2), DP + CTX)
    tok = P(DP, CTX, None)
    own = P(CTX, None, None)
    return jax.shard_map(
        per_device,
        mesh=fine,
        in_specs=(tok, tok, P(), P(), own, own),
        out_specs=(tok, tok, P(CTX, None), P(CTX, None), own, own),
        check_vma=False,
    )
```

time: 223 us -> 213 us (0.955)
  the two profiles are of different devices: /device:TPU:2 before, /device:TPU:32 now
where the time goes in v3:
time: 213 us; the launch traced here: 212 us
  waiting for transfers between devices  101 us (47%)
  starting transfers between devices  60.4 us (28%)
  local copies, waits for them, and re-layouts  20.7 us (10%)
  Pallas kernels  12 us (6%)
  matrix products  8.94 us (4%)
  other arithmetic  8.35 us (4%)
    all_to_all x5, waiting for transfers between devices, swap(): return lax.all_to_all(blocks, axes, 0, 0, tiled=True)  98.9 us
    all_to_all x5, starting transfers between devices, swap(): return lax.all_to_all(blocks, axes, 0, 0, tiled=True)  38.7 us
    ppermute x6, starting transfers between devices, shift(): return lax.ppermute(block, axis, [(i, (i + step) % n) for i in range(n)])  21.6 us
    mul x1, local copies, waits for them, and re-layouts, per_device(): right_factor.transpose(2, 0, 1)[:, :, :, None] * same  7.84 us
    mul x1, local copies, waits for them, and re-layouts, per_device(): right_factor.transpose(1, 0, 2)[:, :, :, None] * same  7.77 us
    pallas_call x2, Pallas kernels, from_hbm(): pl.pallas_call(whole, out_shape=out_shape, in_specs=[pl.BlockSpec(memory_...  7.35 us
    mul x1, other arithmetic, per_device(): right_factor.transpose(2, 0, 1)[:, :, :, None] * same  7.13 us
    dot_general x2, matrix products, mm(): return jnp.dot(a, b, preferred_element_type=F32)  4.86 us
  transfers between devices with their start and end apart: 11, of which 6 were waited for; matrix products, arithmetic and copies ran while one was open for 17% of the time, Pallas kernels for 0%

profile of v3, /device:TPU:32, one launch (start us, length us, event | category | flops | bytes accessed | tf_op | source)
XLA Modules:
  0.0 211.9 jit_solution(11579716000265329657)
XLA Ops:
  0.6 3.4 %shard_map.109 = bf16[32,32,512]{2,1,0:T(8,128)(2,1)} custom-call(bf16[512,512]{1,0:T(8,128)(2,1)} %bitcast.74, bf16[512,512]{1,0:T(8,128)(2,1)} %bitcast.71, bf16[512,512]{1,0:T(8,128)(2,1)} %refs_2_.1, bf16[512,512]{1,0:T(8,128)(2,1)} %bitcast.75, bf16[512,512]{1,0:T(8,128)(2,1)} %refs_4_.1), custom_call_target="tpu_custom_call" | custom-call | tf_op jit(solution)/shard_map/pallas_call | solution.py:75
  4.1 17.2 %all-to-all-start = ((bf16[32,32,512]{2,1,0:T(8,128)(2,1)}), bf16[32,32,512]{2,1,0:T(8,128)(2,1)S(1)}, u32[]{:S(2)}, u32[]{:S(2)}) async-start(bf16[32,32,512]{2,1,0:T(8,128)(2,1)} %shard_map.109), calls=%async_computation | async-start | bytes 2097152 | tf_op jit(solution)/shard_map/all_to_all | solution.py:31
  21.6 7.1 %broadcast_multiply_fusion = (bf16[32,16,32,16]{3,2,1,0:T(8,128)(2,1)}, bf16[32,16,32,16]{3,2,1,0:T(8,128)(2,1)}) fusion(bf16[32,16,32]{2,1,0:T(8,128)(2,1)S(1)} %copy.18, bf16[16,16]{1,0:T(8,128)(2,1)S(1)} %fusion.9, bf16[32,16,32]{2,1,0:T(8,128)(2,1)S(1)} %copy.17), kind=kLoop, calls=%fused_computation | loop fusion | flops 524288 | bytes 1114624 | tf_op jit(solution)/shard_map/mul | solution.py:177
  28.7 7.8 %mul.49.wide = bf16[512,512]{1,0:T(8,128)(2,1)S(1)} reshape(bf16[32,16,32,16]{3,2,1,0:T(8,128)(2,1)} %get-tuple-element.44) | data formatting | bytes 1048576 | tf_op jit(solution)/shard_map/mul | solution.py:176
  36.5 7.8 %mul.52.wide_t = bf16[512,512]{1,0:T(8,128)(2,1)S(1)} reshape(bf16[32,16,32,16]{3,2,1,0:T(8,128)(2,1)} %get-tuple-element.43) | data formatting | bytes 1048576 | tf_op jit(solution)/shard_map/mul | solution.py:177
  44.4 32.0 %all-to-all-done.moved = bf16[32,32,512]{2,1,0:T(8,128)(2,1)S(1)} async-done(((bf16[32,32,512]{2,1,0:T(8,128)(2,1)}), bf16[32,32,512]{2,1,0:T(8,128)(2,1)S(1)}, u32[]{:S(2)}, u32[]{:S(2)}) %all-to-all-start) | async-done | bytes 1048608 | tf_op jit(solution)/shard_map/all_to_all | solution.py:31
  76.4 1.8 shard_map.110
  78.2 5.8 %all-to-all-start.1 = ((bf16[32,32,512]{2,1,0:T(8,128)(2,1)}), bf16[32,32,512]{2,1,0:T(8,128)(2,1)S(1)}, u32[]{:S(2)}, u32[]{:S(2)}) async-start(bf16[32,32,512]{2,1,0:T(8,128)(2,1)} %get-tuple-element.15), calls=%async_computation.1 | async-start | bytes 2097152 | tf_op jit(solution)/shard_map/all_to_all | solution.py:31
  84.0 2.6 %fusion.4 = (f32[512,512]{1,0:T(8,128)}, f32[512,512]{1,0:T(8,128)S(1)}) fusion(bf16[512,512]{1,0:T(8,128)(2,1)} %refs_2_.1, bf16[1,512,512]{2,1,0:T(8,128)(2,1)S(1)} %copy-done.1), kind=kOutput, calls=%fused_computation.13 | convolution fusion | flops 269484032 | bytes 3145728 | tf_op jit(solution)/shard_map/dot_general | solution.py:19
  86.6 1.6 convolution_multiply_fusion.refs_2_
  88.3 50.8 %all-to-all-done.1.refs_0_ = bf16[32,32,512]{2,1,0:T(8,128)(2,1)S(1)} async-done(((bf16[32,32,512]{2,1,0:T(8,128)(2,1)}), bf16[32,32,512]{2,1,0:T(8,128)(2,1)S(1)}, u32[]{:S(2)}, u32[]{:S(2)}) %all-to-all-start.1) | async-done | bytes 1048608 | tf_op jit(solution)/shard_map/all_to_all | solution.py:31
  139.1 1.0 copy-done
  140.1 3.9 %shard_map.111 = (bf16[512,512]{1,0:T(8,128)(2,1)}, bf16[512,512]{1,0:T(8,128)(2,1)}, bf16[8,4,4,8,512]{4,3,2,1,0:T(8,128)(2,1)}) custom-call(bf16[32,32,512]{2,1,0:T(8,128)(2,1)} %copy-done, f32[512,512]{1,0:T(8,128)} %get-tuple-element.45.refs_1_, f32[512,512]{1,0:T(8,128)} %convolution_multiply_fusion.refs_2_, bf16[512,512]{1,0:T(8,128)(2,1)} %bitcast.72, ...), custom_call_target="tpu_custom_call" | custom-call | tf_op jit(solution)/shard_map/pallas_call | solution.py:75
  144.0 5.4 %all-to-all-start.2 = ((bf16[8,128,512]{2,1,0:T(8,128)(2,1)}), bf16[8,128,512]{2,1,0:T(8,128)(2,1)S(1)}, u32[]{:S(2)}, u32[]{:S(2)}) async-start(bf16[8,128,512]{2,1,0:T(8,128)(2,1)} %bitcast.77), calls=%async_computation.2 | async-start | bytes 2097152 | tf_op jit(solution)/shard_map/all_to_all | solution.py:31
  149.5 1.1 slice.8
  151.9 2.3 %collective-permute-start.2 = (bf16[4,40,512]{2,1,0:T(8,128)(2,1)}, bf16[4,40,512]{2,1,0:T(8,128)(2,1)}, u32[]{:S(2)}, u32[]{:S(2)}) collective-permute-start(bf16[4,40,512]{2,1,0:T(8,128)(2,1)} %get-tuple-element.38), channel_id=1, source_target_pairs={{0,32},{32,64},{64,96},{96,0},{1,33},{33,65},{65,97},{97,1},{2,34}... | collective-permute-start | bytes 491528 | tf_op jit(solution)/shard_map/ppermute | solution.py:36
  154.2 5.8 %collective-permute-start.1 = (bf16[4,40,512]{2,1,0:T(8,128)(2,1)}, bf16[4,40,512]{2,1,0:T(8,128)(2,1)}, u32[]{:S(2)}, u32[]{:S(2)}) collective-permute-start(bf16[4,40,512]{2,1,0:T(8,128)(2,1)} %get-tuple-element.37), channel_id=1, source_target_pairs={{0,64},{32,96},{64,0},{96,32},{1,65},{33,97},{65,1},{97,33},{2,66}... | collective-permute-start | bytes 491528 | tf_op jit(solution)/shard_map/ppermute | solution.py:36
  160.0 2.6 %collective-permute-start = (bf16[4,40,512]{2,1,0:T(8,128)(2,1)S(1)}, bf16[4,40,512]{2,1,0:T(8,128)(2,1)}, u32[]{:S(2)}, u32[]{:S(2)}) collective-permute-start(bf16[4,40,512]{2,1,0:T(8,128)(2,1)S(1)} %get-tuple-element.36), channel_id=1, source_target_pairs={{0,96},{32,0},{64,32},{96,64},{1,97},{33,1},{65,33},{97,65},{2,98}... | collective-permute-start | bytes 491528 | tf_op jit(solution)/shard_map/ppermute | solution.py:36
  162.6 2.7 %all-to-all-done.2.parts = bf16[8,128,512]{2,1,0:T(8,128)(2,1)S(1)} async-done(((bf16[8,128,512]{2,1,0:T(8,128)(2,1)}), bf16[8,128,512]{2,1,0:T(8,128)(2,1)S(1)}, u32[]{:S(2)}, u32[]{:S(2)}) %all-to-all-start.2) | async-done | bytes 1048608 | tf_op jit(solution)/shard_map/all_to_all | solution.py:31
  166.1 3.5 %all-to-all-start.3 = ((bf16[16,8,512]{2,1,0:T(8,128)(2,1)}), bf16[16,8,512]{2,1,0:T(8,128)(2,1)S(1)}, u32[]{:S(2)}, u32[]{:S(2)}) async-start(bf16[16,8,512]{2,1,0:T(8,128)(2,1)} %bitcast.21), calls=%async_computation.3 | async-start | bytes 262144 | tf_op jit(solution)/shard_map/all_to_all | solution.py:31
  169.6 1.2 fusion.8
  170.8 2.1 collective-permute-start.3
  172.9 4.7 %collective-permute-start.4 = (bf16[40,512]{1,0:T(8,128)(2,1)S(1)}, bf16[40,512]{1,0:T(8,128)(2,1)S(1)}, u32[]{:S(2)}, u32[]{:S(2)}) collective-permute-start(bf16[40,512]{1,0:T(8,128)(2,1)S(1)} %get-tuple-element.40), channel_id=1, source_target_pairs={{0,256},{128,384},{256,0},{384,128},{1,257},{129,385},{257,1},{385... | collective-permute-start | bytes 122888 | tf_op jit(solution)/shard_map/ppermute | solution.py:36
  177.6 4.3 %collective-permute-start.5 = (bf16[40,512]{1,0:T(8,128)(2,1)S(1)}, bf16[40,512]{1,0:T(8,128)(2,1)S(1)}, u32[]{:S(2)}, u32[]{:S(2)}) collective-permute-start(bf16[40,512]{1,0:T(8,128)(2,1)S(1)} %get-tuple-element.39), channel_id=1, source_target_pairs={{0,128},{128,256},{256,384},{384,0},{1,129},{129,257},{257,385},{3... | collective-permute-start | bytes 122888 | tf_op jit(solution)/shard_map/ppermute | solution.py:36
  181.9 1.6 collective-permute-done.5.three
  184.0 1.0 shard_map.113
  184.9 6.9 %all-to-all-start.4 = ((bf16[16,48,512]{2,1,0:T(8,128)(2,1)}), bf16[16,48,512]{2,1,0:T(8,128)(2,1)S(1)}, u32[]{:S(2)}, u32[]{:S(2)}) async-start(bf16[16,48,512]{2,1,0:T(8,128)(2,1)} %shard_map.113), calls=%async_computation.4 | async-start | bytes 1572864 | tf_op jit(solution)/shard_map/all_to_all | solution.py:31
  192.3 1.5 fusion.2
  193.8 1.0 copy.23
  194.8 2.3 %fusion.3 = bf16[1,512,512]{2,1,0:T(8,128)(2,1)} fusion(bf16[512,512]{1,0:T(8,128)(2,1)} %get-tuple-element.16, bf16[512,512]{1,0:T(8,128)(2,1)S(1)} %copy-done.5), kind=kOutput, calls=%fused_computation.11 | convolution fusion | flops 268697600 | bytes 1572864 | tf_op jit(solution)/shard_map/dot_general | solution.py:19
  197.1 12.9 %all-to-all-done.4.packed = bf16[16,48,512]{2,1,0:T(8,128)(2,1)S(1)} async-done(((bf16[16,48,512]{2,1,0:T(8,128)(2,1)}), bf16[16,48,512]{2,1,0:T(8,128)(2,1)S(1)}, u32[]{:S(2)}, u32[]{:S(2)}) %all-to-all-start.4) | async-done | bytes 786464 | tf_op jit(solution)/shard_map/all_to_all | solution.py:31
  210.0 1.1 shard_map.114
  (35 shorter events, 4.3 us)
Async XLA Ops:
  0.6 20.7 %copy-start.8 = (bf16[16,32,32]{2,1,0:T(8,128)(2,1)S(1)}, bf16[16,32,32]{2,1,0:T(8,128)(2,1)}, u32[]{:S(2)}) copy-start(bf16[16,32,32]{2,1,0:T(8,128)(2,1)} %param.11) | copy-start | bytes 98308
  4.1 72.3 %all-to-all-start = ((bf16[32,32,512]{2,1,0:T(8,128)(2,1)}), bf16[32,32,512]{2,1,0:T(8,128)(2,1)S(1)}, u32[]{:S(2)}, u32[]{:S(2)}) async-start(bf16[32,32,512]{2,1,0:T(8,128)(2,1)} %shard_map.109), calls=%async_computation | async-start | bytes 2097152 | tf_op jit(solution)/shard_map/all_to_all | solution.py:31
  36.5 47.5 %copy-start.1 = (bf16[1,512,512]{2,1,0:T(8,128)(2,1)S(1)}, bf16[1,512,512]{2,1,0:T(8,128)(2,1)}, u32[]{:S(2)}) copy-start(bf16[1,512,512]{2,1,0:T(8,128)(2,1)} %param.6) | copy-start | bytes 1572868
  78.2 8.4 %copy-start.4 = (bf16[512,512]{1,0:T(8,128)(2,1)S(1)}, bf16[512,512]{1,0:T(8,128)(2,1)}, u32[]{:S(2)}) copy-start(bf16[512,512]{1,0:T(8,128)(2,1)} %refs_4_.1) | copy-start | bytes 1572868
  78.2 8.4 %copy-start.7 = (bf16[1,512,512]{2,1,0:T(8,128)(2,1)S(1)}, bf16[1,512,512]{2,1,0:T(8,128)(2,1)}, u32[]{:S(2)}) copy-start(bf16[1,512,512]{2,1,0:T(8,128)(2,1)} %param.7) | copy-start | bytes 1572868
  78.2 60.9 %all-to-all-start.1 = ((bf16[32,32,512]{2,1,0:T(8,128)(2,1)}), bf16[32,32,512]{2,1,0:T(8,128)(2,1)S(1)}, u32[]{:S(2)}, u32[]{:S(2)}) async-start(bf16[32,32,512]{2,1,0:T(8,128)(2,1)} %get-tuple-element.15), calls=%async_computation.1 | async-start | bytes 2097152 | tf_op jit(solution)/shard_map/all_to_all | solution.py:31
  88.2 62.3 %copy-start.2 = (bf16[1,512,512]{2,1,0:T(8,128)(2,1)S(1)}, bf16[1,512,512]{2,1,0:T(8,128)(2,1)}, u32[]{:S(2)}) copy-start(bf16[1,512,512]{2,1,0:T(8,128)(2,1)} %param.6) | copy-start | bytes 1572868
  139.1 1.0 copy-start
  144.0 21.3 %all-to-all-start.2 = ((bf16[8,128,512]{2,1,0:T(8,128)(2,1)}), bf16[8,128,512]{2,1,0:T(8,128)(2,1)S(1)}, u32[]{:S(2)}, u32[]{:S(2)}) async-start(bf16[8,128,512]{2,1,0:T(8,128)(2,1)} %bitcast.77), calls=%async_computation.2 | async-start | bytes 2097152 | tf_op jit(solution)/shard_map/all_to_all | solution.py:31
  151.1 40.7 %copy-start.6 = (bf16[1,512,512]{2,1,0:T(8,128)(2,1)S(1)}, bf16[1,512,512]{2,1,0:T(8,128)(2,1)}, u32[]{:S(2)}) copy-start(bf16[1,512,512]{2,1,0:T(8,128)(2,1)} %param.10) | copy-start | bytes 1572868
  151.1 41.1 %copy-start.3 = (bf16[512,512]{1,0:T(8,128)(2,1)S(1)}, bf16[512,512]{1,0:T(8,128)(2,1)}, u32[]{:S(2)}) copy-start(bf16[512,512]{1,0:T(8,128)(2,1)} %refs_2_.1) | copy-start | bytes 1572868
  151.9 17.7 %collective-permute-start.2 = (bf16[4,40,512]{2,1,0:T(8,128)(2,1)}, bf16[4,40,512]{2,1,0:T(8,128)(2,1)}, u32[]{:S(2)}, u32[]{:S(2)}) collective-permute-start(bf16[4,40,512]{2,1,0:T(8,128)(2,1)} %get-tuple-element.38), channel_id=1, source_target_pairs={{0,32},{32,64},{64,96},{96,0},{1,33},{33,65},{65,97},{97,1},{2,34}... | collective-permute-start | bytes 491528 | tf_op jit(solution)/shard_map/ppermute | solution.py:36
  154.2 15.4 %collective-permute-start.1 = (bf16[4,40,512]{2,1,0:T(8,128)(2,1)}, bf16[4,40,512]{2,1,0:T(8,128)(2,1)}, u32[]{:S(2)}, u32[]{:S(2)}) collective-permute-start(bf16[4,40,512]{2,1,0:T(8,128)(2,1)} %get-tuple-element.37), channel_id=1, source_target_pairs={{0,64},{32,96},{64,0},{96,32},{1,65},{33,97},{65,1},{97,33},{2,66}... | collective-permute-start | bytes 491528 | tf_op jit(solution)/shard_map/ppermute | solution.py:36
  160.0 9.6 %collective-permute-start = (bf16[4,40,512]{2,1,0:T(8,128)(2,1)S(1)}, bf16[4,40,512]{2,1,0:T(8,128)(2,1)}, u32[]{:S(2)}, u32[]{:S(2)}) collective-permute-start(bf16[4,40,512]{2,1,0:T(8,128)(2,1)S(1)} %get-tuple-element.36), channel_id=1, source_target_pairs={{0,96},{32,0},{64,32},{96,64},{1,97},{33,1},{65,33},{97,65},{2,98}... | collective-permute-start | bytes 491528 | tf_op jit(solution)/shard_map/ppermute | solution.py:36
  166.1 17.9 %all-to-all-start.3 = ((bf16[16,8,512]{2,1,0:T(8,128)(2,1)}), bf16[16,8,512]{2,1,0:T(8,128)(2,1)S(1)}, u32[]{:S(2)}, u32[]{:S(2)}) async-start(bf16[16,8,512]{2,1,0:T(8,128)(2,1)} %bitcast.21), calls=%async_computation.3 | async-start | bytes 262144 | tf_op jit(solution)/shard_map/all_to_all | solution.py:31
  170.8 11.0 %collective-permute-start.3 = (bf16[40,512]{1,0:T(8,128)(2,1)S(1)}, bf16[40,512]{1,0:T(8,128)(2,1)S(1)}, u32[]{:S(2)}, u32[]{:S(2)}) collective-permute-start(bf16[40,512]{1,0:T(8,128)(2,1)S(1)} %get-tuple-element.41), channel_id=1, source_target_pairs={{0,384},{128,0},{256,128},{384,256},{1,385},{129,1},{257,129},{385... | collective-permute-start | bytes 122888 | tf_op jit(solution)/shard_map/ppermute | solution.py:36
  172.9 9.0 %collective-permute-start.4 = (bf16[40,512]{1,0:T(8,128)(2,1)S(1)}, bf16[40,512]{1,0:T(8,128)(2,1)S(1)}, u32[]{:S(2)}, u32[]{:S(2)}) collective-permute-start(bf16[40,512]{1,0:T(8,128)(2,1)S(1)} %get-tuple-element.40), channel_id=1, source_target_pairs={{0,256},{128,384},{256,0},{384,128},{1,257},{129,385},{257,1},{385... | collective-permute-start | bytes 122888 | tf_op jit(solution)/shard_map/ppermute | solution.py:36
  177.6 5.9 %collective-permute-start.5 = (bf16[40,512]{1,0:T(8,128)(2,1)S(1)}, bf16[40,512]{1,0:T(8,128)(2,1)S(1)}, u32[]{:S(2)}, u32[]{:S(2)}) collective-permute-start(bf16[40,512]{1,0:T(8,128)(2,1)S(1)} %get-tuple-element.39), channel_id=1, source_target_pairs={{0,128},{128,256},{256,384},{384,0},{1,129},{129,257},{257,385},{3... | collective-permute-start | bytes 122888 | tf_op jit(solution)/shard_map/ppermute | solution.py:36
  184.0 10.8 %copy-start.5 = (bf16[512,512]{1,0:T(8,128)(2,1)S(1)}, bf16[512,512]{1,0:T(8,128)(2,1)}, u32[]{:S(2)}) copy-start(bf16[512,512]{1,0:T(8,128)(2,1)} %refs_4_.1) | copy-start | bytes 1572868
  184.9 25.0 %all-to-all-start.4 = ((bf16[16,48,512]{2,1,0:T(8,128)(2,1)}), bf16[16,48,512]{2,1,0:T(8,128)(2,1)S(1)}, u32[]{:S(2)}, u32[]{:S(2)}) async-start(bf16[16,48,512]{2,1,0:T(8,128)(2,1)} %shard_map.113), calls=%async_computation.4 | async-start | bytes 1572864 | tf_op jit(solution)/shard_map/all_to_all | solution.py:31

commit v4 on v3

--- a/solution.py
+++ b/solution.py
@@ -110,22 +110,6 @@
     right[...] = mm(kept, choose).astype(BF)
 
 
-def gate_body(ready, back, activated, sloped, x, cot, hidden, grad_gate_pre, terms):
-    tok, ch = x.shape
-    yc, nl, nz, part, _ = terms.shape
-    pos = back.shape[1] // 2
-    ready(0, 1, 2)
-    mixed = back[:, :pos].reshape(tok, ch).astype(F32)
-    grad_gate_pre[...] = (mixed * sloped[...]).astype(BF)
-    hidden[...] = (mixed * activated[...]).astype(BF)
-    ready(3, 4)
-    for i, term in enumerate((mm_tl(x[...], grad_gate_pre[...]), mm_tl(hidden[...], cot[...]))):
-        term = term.reshape(nz, yc, nl // 2, part, ch)
-        for half in range(nl // 2):
-            for z in range(nz):
-                terms[:, i * (nl // 2) + half, z] = term[z, :, half].astype(BF)
-
-
 def sum_body(parts, total):
     total[...] = parts[...].astype(F32).sum(0).astype(BF)
 
@@ -142,7 +126,8 @@
     size = left.shape[0] // seqs
     left[...] = packed[:, :size].astype(F32).reshape(left.shape) * factor_scale
     rest = packed[:, size:].astype(F32)
-    right[...] = rest[:, :8, :128] * factor_scale
+    for g in range(right.shape[1] // 8):
+        right[:, 8 * g : 8 * (g + 1)] = rest[:, :8, 128 * g : 128 * g + right.shape[2]] * factor_scale
     share = gate.shape[0]
     terms = rest[:, 8:].reshape(-1, 4, 8, ch).sum(1).reshape(2 * share, ch) * weight_scale
     gate[...] = terms[:share]
@@ -179,14 +164,18 @@
     sent, term_right = in_vmem(middle_body, (pair, right_shape), moved, wide, wide_t)
     back = swap(sent, CTX)
 
-    term_right = term_right[:, :nb].reshape(nb, pos, nb).transpose(1, 0, 2).reshape(nl, nx, -1, 128)
-    term_right = jnp.pad(term_right, ((0, 0), (0, 0), (0, 0), (0, ch - 128)))
+    term_right = term_right.reshape(nb // 8, 8, pos, 128).transpose(2, 1, 0, 3).reshape(nl, nx, 8, ch)
 
     share = ch // ctx
     yc = lax.axis_size(YC)
-    token_pair = jax.ShapeDtypeStruct((tok, ch), BF)
-    gated = (token_pair, token_pair, jax.ShapeDtypeStruct((yc, nl, nz, 2 * share // nl, ch), BF))
-    hidden, grad_gate_pre, terms = from_hbm(gate_body, gated, back, activated, grad_hidden * slope, x, cot)
+    mixed = back[:, :pos].reshape(tok, ch).astype(F32)
+    hidden = (mixed * activated).astype(BF)
+    grad_gate_pre = (grad_hidden * mixed * slope).astype(BF)
+
+    def by_yc(term):
+        return term.astype(BF).reshape(nz, yc, nl // 2, -1, ch).transpose(1, 2, 0, 3, 4)
+
+    terms = jnp.concatenate([by_yc(mm_tl(x, grad_gate_pre)), by_yc(mm_tl(hidden, cot))], 1)
     initial_gradient = back[:, pos:].reshape(tok, ch)
 
     terms = swap(terms.reshape(yc, nz * 2 * share, ch), YC)
@@ -207,7 +196,7 @@
         jax.ShapeDtypeStruct((tok, tok), F32),
         jax.ShapeDtypeStruct((share, ch), F32),
         jax.ShapeDtypeStruct((share, ch), F32),
-        jax.ShapeDtypeStruct((seqs, 8, 128), F32),
+        jax.ShapeDtypeStruct((pos, nb, nb), F32),
     )
     finish = functools.partial(finish_body, weight_scale, factor_scale)
     sum_left, sum_gate, sum_out, sum_right = in_vmem(finish, finished, packed)
@@ -220,7 +209,7 @@
         sum_gate,
         sum_out,
         sum_left[None],
-        sum_right.reshape(pos, nb, nb),
+        sum_right,
     )
 
 

time: 213 us -> 211 us (level)
  blocking collectives: 0 us -> 60.6 us
  waiting for transfers between devices: 101 us -> 52.2 us
  starting transfers between devices: 60.4 us -> 53.5 us
  Pallas kernels: 12 us -> 7.58 us
  local copies, waits for them, and re-layouts: 20.7 us -> 18.3 us
    all_to_all x0 -> x1, blocking collectives: none -> 60.6 us  [swap(): return lax.all_to_all(blocks, axes, 0, 0, tiled=True)]
    all_to_all x5 -> x4, waiting for transfers between devices: 98.9 us -> 50.5 us  [swap(): return lax.all_to_all(blocks, axes, 0, 0, tiled=True)]
    all_to_all x5 -> x4, starting transfers between devices: 38.7 us -> 32.9 us  [swap(): return lax.all_to_all(blocks, axes, 0, 0, tiled=True)]
    pallas_call x2 -> x1, Pallas kernels: 7.35 us -> 3.44 us  [from_hbm(): pl.pallas_call(whole, out_shape=out_shape, in_specs=[pl.BlockSpec(memory_...]
    dot_general x2, matrix products: 4.86 us -> 1.82 us  [mm(): return jnp.dot(a, b, preferred_element_type=F32)]
  transfers between devices with their start and end apart: 11 -> 10, of which waited for: 6 -> 5; matrix products, arithmetic and copies ran while one was open for 17% -> 15% of each run, Pallas kernels for 0% -> 0%
where the time goes in v4:
time: 211 us; the launch traced here: 210 us
  blocking collectives  60.6 us (29%)
  starting transfers between devices  53.5 us (25%)
  waiting for transfers between devices  52.2 us (25%)
  local copies, waits for them, and re-layouts  18.3 us (9%)
  other arithmetic  10 us (5%)
  Pallas kernels  7.58 us (4%)
  matrix products  6.91 us (3%)
    all_to_all x1, blocking collectives, swap(): return lax.all_to_all(blocks, axes, 0, 0, tiled=True)  60.6 us
    all_to_all x4, waiting for transfers between devices, swap(): return lax.all_to_all(blocks, axes, 0, 0, tiled=True)  50.5 us
    all_to_all x4, starting transfers between devices, swap(): return lax.all_to_all(blocks, axes, 0, 0, tiled=True)  32.9 us
    ppermute x6, starting transfers between devices, shift(): return lax.ppermute(block, axis, [(i, (i + step) % n) for i in range(n)])  20.6 us
    mul x1, local copies, waits for them, and re-layouts, per_device(): right_factor.transpose(2, 0, 1)[:, :, :, None] * same  7.78 us
    mul x1, local copies, waits for them, and re-layouts, per_device(): right_factor.transpose(1, 0, 2)[:, :, :, None] * same  7.77 us
    mul x1, other arithmetic, per_device(): right_factor.transpose(2, 0, 1)[:, :, :, None] * same  7.13 us
  transfers between devices with their start and end apart: 10, of which 5 were waited for; matrix products, arithmetic and copies ran while one was open for 15% of the time, Pallas kernels for 0%

profile of v4, /device:TPU:32, one launch (start us, length us, event | category | flops | bytes accessed | tf_op | source)
XLA Modules:
  0.0 210.0 jit_solution(1513967255610083683)
XLA Ops:
  0.6 3.4 %shard_map.109 = bf16[32,32,512]{2,1,0:T(8,128)(2,1)} custom-call(bf16[512,512]{1,0:T(8,128)(2,1)} %bitcast.93, bf16[512,512]{1,0:T(8,128)(2,1)} %bitcast.87, bf16[512,512]{1,0:T(8,128)(2,1)} %refs_2_.1, bf16[512,512]{1,0:T(8,128)(2,1)} %bitcast.97, bf16[512,512]{1,0:T(8,128)(2,1)} %refs_4_.1), custom_call_target="tpu_custom_call" | custom-call | tf_op jit(solution)/shard_map/pallas_call | solution.py:75
  4.1 17.2 %all-to-all-start = ((bf16[32,32,512]{2,1,0:T(8,128)(2,1)}), bf16[32,32,512]{2,1,0:T(8,128)(2,1)S(1)}, u32[]{:S(2)}, u32[]{:S(2)}) async-start(bf16[32,32,512]{2,1,0:T(8,128)(2,1)} %shard_map.109), calls=%async_computation | async-start | bytes 2097152 | tf_op jit(solution)/shard_map/all_to_all | solution.py:31
  21.6 7.1 %broadcast_multiply_fusion = (bf16[32,16,32,16]{3,2,1,0:T(8,128)(2,1)}, bf16[32,16,32,16]{3,2,1,0:T(8,128)(2,1)}) fusion(bf16[32,16,32]{2,1,0:T(8,128)(2,1)S(1)} %copy.20, bf16[16,16]{1,0:T(8,128)(2,1)S(1)} %fusion.17, bf16[32,16,32]{2,1,0:T(8,128)(2,1)S(1)} %copy.19), kind=kLoop, calls=%fused_computation | loop fusion | flops 524288 | bytes 1114624 | tf_op jit(solution)/shard_map/mul | solution.py:162
  28.7 7.8 %mul.55.wide = bf16[512,512]{1,0:T(8,128)(2,1)S(1)} reshape(bf16[32,16,32,16]{3,2,1,0:T(8,128)(2,1)} %get-tuple-element.40) | data formatting | bytes 1048576 | tf_op jit(solution)/shard_map/mul | solution.py:161
  36.5 7.8 %mul.58.wide_t = bf16[512,512]{1,0:T(8,128)(2,1)S(1)} reshape(bf16[32,16,32,16]{3,2,1,0:T(8,128)(2,1)} %get-tuple-element.39) | data formatting | bytes 1048576 | tf_op jit(solution)/shard_map/mul | solution.py:162
  44.3 32.1 %all-to-all-done.moved = bf16[32,32,512]{2,1,0:T(8,128)(2,1)S(1)} async-done(((bf16[32,32,512]{2,1,0:T(8,128)(2,1)}), bf16[32,32,512]{2,1,0:T(8,128)(2,1)S(1)}, u32[]{:S(2)}, u32[]{:S(2)}) %all-to-all-start) | async-done | bytes 1048608 | tf_op jit(solution)/shard_map/all_to_all | solution.py:31
  76.4 1.2 shard_map.110
  77.6 60.6 %all_to_all.25 = bf16[32,32,512]{2,1,0:T(8,128)(2,1)S(1)} all-to-all(bf16[32,32,512]{2,1,0:T(8,128)(2,1)S(1)} %get-tuple-element.12), channel_id=1, replica_groups=mesh['zl'=4,'x'=4,'zh'=4,'y'=4,'c'=2] {'zh','y','c'}, dimensions={0} | all-to-all | bytes 2097152 | tf_op jit(solution)/shard_map/all_to_all | solution.py:31
  139.4 0.7 fusion.1
  140.1 0.8 copy-done.5
  141.9 1.1 pad_maximum_fusion
  143.0 5.3 %all-to-all-start.2 = ((bf16[8,128,512]{2,1,0:T(8,128)(2,1)}), bf16[8,128,512]{2,1,0:T(8,128)(2,1)S(1)}, u32[]{:S(2)}, u32[]{:S(2)}) async-start(bf16[8,128,512]{2,1,0:T(8,128)(2,1)} %bitcast.92), calls=%async_computation.2 | async-start | bytes 2097152 | tf_op jit(solution)/shard_map/all_to_all | solution.py:31
  148.8 0.7 fusion.14
  149.6 4.8 %collective-permute-start = (bf16[4,40,512]{2,1,0:T(8,128)(2,1)}, bf16[4,40,512]{2,1,0:T(8,128)(2,1)S(1)}, u32[]{:S(2)}, u32[]{:S(2)}) collective-permute-start(bf16[4,40,512]{2,1,0:T(8,128)(2,1)} %get-tuple-element.32), channel_id=1, source_target_pairs={{0,96},{32,0},{64,32},{96,64},{1,97},{33,1},{65,33},{97,65},{2,98}... | collective-permute-start | bytes 491528 | tf_op jit(solution)/shard_map/ppermute | solution.py:36
  154.4 1.9 collective-permute-start.1
  156.3 2.9 %collective-permute-start.2 = (bf16[4,40,512]{2,1,0:T(8,128)(2,1)S(1)}, bf16[4,40,512]{2,1,0:T(8,128)(2,1)}, u32[]{:S(2)}, u32[]{:S(2)}) collective-permute-start(bf16[4,40,512]{2,1,0:T(8,128)(2,1)S(1)} %get-tuple-element.34), channel_id=1, source_target_pairs={{0,32},{32,64},{64,96},{96,0},{1,33},{33,65},{65,97},{97,1},{2,34}... | collective-permute-start | bytes 491528 | tf_op jit(solution)/shard_map/ppermute | solution.py:36
  159.2 5.1 %all-to-all-done.2.parts = bf16[8,128,512]{2,1,0:T(8,128)(2,1)S(1)} async-done(((bf16[8,128,512]{2,1,0:T(8,128)(2,1)}), bf16[8,128,512]{2,1,0:T(8,128)(2,1)S(1)}, u32[]{:S(2)}, u32[]{:S(2)}) %all-to-all-start.2) | async-done | bytes 1048608 | tf_op jit(solution)/shard_map/all_to_all | solution.py:31
  164.3 0.8 shard_map.111
  165.1 3.5 %all-to-all-start.3 = ((bf16[16,8,512]{2,1,0:T(8,128)(2,1)}), bf16[16,8,512]{2,1,0:T(8,128)(2,1)S(1)}, u32[]{:S(2)}, u32[]{:S(2)}) async-start(bf16[16,8,512]{2,1,0:T(8,128)(2,1)} %bitcast.30), calls=%async_computation.3 | async-start | bytes 262144 | tf_op jit(solution)/shard_map/all_to_all | solution.py:31
  168.6 1.1 fusion.8
  169.8 2.1 collective-permute-start.3
  171.8 4.7 %collective-permute-start.4 = (bf16[40,512]{1,0:T(8,128)(2,1)S(1)}, bf16[40,512]{1,0:T(8,128)(2,1)S(1)}, u32[]{:S(2)}, u32[]{:S(2)}) collective-permute-start(bf16[40,512]{1,0:T(8,128)(2,1)S(1)} %get-tuple-element.36), channel_id=1, source_target_pairs={{0,256},{128,384},{256,0},{384,128},{1,257},{129,385},{257,1},{385... | collective-permute-start | bytes 122888 | tf_op jit(solution)/shard_map/ppermute | solution.py:36
  176.5 4.3 %collective-permute-start.5 = (bf16[40,512]{1,0:T(8,128)(2,1)S(1)}, bf16[40,512]{1,0:T(8,128)(2,1)S(1)}, u32[]{:S(2)}, u32[]{:S(2)}) collective-permute-start(bf16[40,512]{1,0:T(8,128)(2,1)S(1)} %get-tuple-element.35), channel_id=1, source_target_pairs={{0,128},{128,256},{256,384},{384,0},{1,129},{129,257},{257,385},{3... | collective-permute-start | bytes 122888 | tf_op jit(solution)/shard_map/ppermute | solution.py:36
  180.8 1.6 collective-permute-done.5.three
  182.9 1.0 shard_map.112
  183.9 6.8 %all-to-all-start.4 = ((bf16[16,48,512]{2,1,0:T(8,128)(2,1)}), bf16[16,48,512]{2,1,0:T(8,128)(2,1)S(1)}, u32[]{:S(2)}, u32[]{:S(2)}) async-start(bf16[16,48,512]{2,1,0:T(8,128)(2,1)} %shard_map.112), calls=%async_computation.4 | async-start | bytes 1572864 | tf_op jit(solution)/shard_map/all_to_all | solution.py:31
  190.7 1.5 convolution_bitcast_fusion
  192.2 1.5 fusion.3
  193.8 1.0 copy.27
  194.8 1.2 fusion.4
  196.0 12.8 %all-to-all-done.4.packed = bf16[16,48,512]{2,1,0:T(8,128)(2,1)S(1)} async-done(((bf16[16,48,512]{2,1,0:T(8,128)(2,1)}), bf16[16,48,512]{2,1,0:T(8,128)(2,1)S(1)}, u32[]{:S(2)}, u32[]{:S(2)}) %all-to-all-start.4) | async-done | bytes 786464 | tf_op jit(solution)/shard_map/all_to_all | solution.py:31
  208.8 1.1 shard_map.113
  (36 shorter events, 3.5 us)
Async XLA Ops:
  0.6 20.7 %copy-start.9 = (bf16[16,32,32]{2,1,0:T(8,128)(2,1)S(1)}, bf16[16,32,32]{2,1,0:T(8,128)(2,1)}, u32[]{:S(2)}) copy-start(bf16[16,32,32]{2,1,0:T(8,128)(2,1)} %param.11) | copy-start | bytes 98308
  4.1 72.3 %all-to-all-start = ((bf16[32,32,512]{2,1,0:T(8,128)(2,1)}), bf16[32,32,512]{2,1,0:T(8,128)(2,1)S(1)}, u32[]{:S(2)}, u32[]{:S(2)}) async-start(bf16[32,32,512]{2,1,0:T(8,128)(2,1)} %shard_map.109), calls=%async_computation | async-start | bytes 2097152 | tf_op jit(solution)/shard_map/all_to_all | solution.py:31
  44.3 94.0 %copy-start = (bf16[1,512,512]{2,1,0:T(8,128)(2,1)S(1)}, bf16[1,512,512]{2,1,0:T(8,128)(2,1)}, u32[]{:S(2)}) copy-start(bf16[1,512,512]{2,1,0:T(8,128)(2,1)} %param.6) | copy-start | bytes 1572868
  76.4 61.9 %copy-start.1 = (bf16[512,512]{1,0:T(8,128)(2,1)S(1)}, bf16[512,512]{1,0:T(8,128)(2,1)}, u32[]{:S(2)}) copy-start(bf16[512,512]{1,0:T(8,128)(2,1)} %refs_2_.1) | copy-start | bytes 1572868
  138.2 1.0 copy-start.3
  138.2 1.2 copy-start.6
  138.9 2.5 %copy-start.7 = (bf16[512,512]{1,0:T(8,128)(2,1)}, bf16[512,512]{1,0:T(8,128)(2,1)S(1)}, u32[]{:S(2)}) copy-start(bf16[512,512]{1,0:T(8,128)(2,1)S(1)} %get-tuple-element.41) | copy-start | bytes 1572868
  140.1 0.8 copy-start.5
  143.0 21.3 %all-to-all-start.2 = ((bf16[8,128,512]{2,1,0:T(8,128)(2,1)}), bf16[8,128,512]{2,1,0:T(8,128)(2,1)S(1)}, u32[]{:S(2)}, u32[]{:S(2)}) async-start(bf16[8,128,512]{2,1,0:T(8,128)(2,1)} %bitcast.92), calls=%async_computation.2 | async-start | bytes 2097152 | tf_op jit(solution)/shard_map/all_to_all | solution.py:31
  149.6 42.7 %copy-start.2 = (bf16[512,512]{1,0:T(8,128)(2,1)S(1)}, bf16[512,512]{1,0:T(8,128)(2,1)}, u32[]{:S(2)}) copy-start(bf16[512,512]{1,0:T(8,128)(2,1)} %refs_2_.1) | copy-start | bytes 1572868
  149.6 19.0 %collective-permute-start = (bf16[4,40,512]{2,1,0:T(8,128)(2,1)}, bf16[4,40,512]{2,1,0:T(8,128)(2,1)S(1)}, u32[]{:S(2)}, u32[]{:S(2)}) collective-permute-start(bf16[4,40,512]{2,1,0:T(8,128)(2,1)} %get-tuple-element.32), channel_id=1, source_target_pairs={{0,96},{32,0},{64,32},{96,64},{1,97},{33,1},{65,33},{97,65},{2,98}... | collective-permute-start | bytes 491528 | tf_op jit(solution)/shard_map/ppermute | solution.py:36
  154.4 14.3 %collective-permute-start.1 = (bf16[4,40,512]{2,1,0:T(8,128)(2,1)S(1)}, bf16[4,40,512]{2,1,0:T(8,128)(2,1)}, u32[]{:S(2)}, u32[]{:S(2)}) collective-permute-start(bf16[4,40,512]{2,1,0:T(8,128)(2,1)S(1)} %get-tuple-element.33), channel_id=1, source_target_pairs={{0,64},{32,96},{64,0},{96,32},{1,65},{33,97},{65,1},{97,33},{2,66}... | collective-permute-start | bytes 491528 | tf_op jit(solution)/shard_map/ppermute | solution.py:36
  156.3 12.3 %collective-permute-start.2 = (bf16[4,40,512]{2,1,0:T(8,128)(2,1)S(1)}, bf16[4,40,512]{2,1,0:T(8,128)(2,1)}, u32[]{:S(2)}, u32[]{:S(2)}) collective-permute-start(bf16[4,40,512]{2,1,0:T(8,128)(2,1)S(1)} %get-tuple-element.34), channel_id=1, source_target_pairs={{0,32},{32,64},{64,96},{96,0},{1,33},{33,65},{65,97},{97,1},{2,34}... | collective-permute-start | bytes 491528 | tf_op jit(solution)/shard_map/ppermute | solution.py:36
  165.1 17.8 %all-to-all-start.3 = ((bf16[16,8,512]{2,1,0:T(8,128)(2,1)}), bf16[16,8,512]{2,1,0:T(8,128)(2,1)S(1)}, u32[]{:S(2)}, u32[]{:S(2)}) async-start(bf16[16,8,512]{2,1,0:T(8,128)(2,1)} %bitcast.30), calls=%async_computation.3 | async-start | bytes 262144 | tf_op jit(solution)/shard_map/all_to_all | solution.py:31
  169.8 11.0 %collective-permute-start.3 = (bf16[40,512]{1,0:T(8,128)(2,1)S(1)}, bf16[40,512]{1,0:T(8,128)(2,1)S(1)}, u32[]{:S(2)}, u32[]{:S(2)}) collective-permute-start(bf16[40,512]{1,0:T(8,128)(2,1)S(1)} %get-tuple-element.37), channel_id=1, source_target_pairs={{0,384},{128,0},{256,128},{384,256},{1,385},{129,1},{257,129},{385... | collective-permute-start | bytes 122888 | tf_op jit(solution)/shard_map/ppermute | solution.py:36
  171.8 9.0 %collective-permute-start.4 = (bf16[40,512]{1,0:T(8,128)(2,1)S(1)}, bf16[40,512]{1,0:T(8,128)(2,1)S(1)}, u32[]{:S(2)}, u32[]{:S(2)}) collective-permute-start(bf16[40,512]{1,0:T(8,128)(2,1)S(1)} %get-tuple-element.36), channel_id=1, source_target_pairs={{0,256},{128,384},{256,0},{384,128},{1,257},{129,385},{257,1},{385... | collective-permute-start | bytes 122888 | tf_op jit(solution)/shard_map/ppermute | solution.py:36
  176.5 5.9 %collective-permute-start.5 = (bf16[40,512]{1,0:T(8,128)(2,1)S(1)}, bf16[40,512]{1,0:T(8,128)(2,1)S(1)}, u32[]{:S(2)}, u32[]{:S(2)}) collective-permute-start(bf16[40,512]{1,0:T(8,128)(2,1)S(1)} %get-tuple-element.35), channel_id=1, source_target_pairs={{0,128},{128,256},{256,384},{384,0},{1,129},{129,257},{257,385},{3... | collective-permute-start | bytes 122888 | tf_op jit(solution)/shard_map/ppermute | solution.py:36
  182.9 11.8 %copy-start.4 = (bf16[512,512]{1,0:T(8,128)(2,1)S(1)}, bf16[512,512]{1,0:T(8,128)(2,1)}, u32[]{:S(2)}) copy-start(bf16[512,512]{1,0:T(8,128)(2,1)} %refs_4_.1) | copy-start | bytes 1572868
  182.9 11.8 %copy-start.8 = (bf16[512,512]{1,0:T(8,128)(2,1)S(1)}, bf16[512,512]{1,0:T(8,128)(2,1)}, u32[]{:S(2)}) copy-start(bf16[512,512]{1,0:T(8,128)(2,1)} %copy-done.7) | copy-start | bytes 1572868
  183.9 24.9 %all-to-all-start.4 = ((bf16[16,48,512]{2,1,0:T(8,128)(2,1)}), bf16[16,48,512]{2,1,0:T(8,128)(2,1)S(1)}, u32[]{:S(2)}, u32[]{:S(2)}) async-start(bf16[16,48,512]{2,1,0:T(8,128)(2,1)} %shard_map.112), calls=%async_computation.4 | async-start | bytes 1572864 | tf_op jit(solution)/shard_map/all_to_all | solution.py:31

commit v5 on v4

--- a/solution.py
+++ b/solution.py
@@ -160,6 +160,8 @@
     same = jnp.eye(pos, dtype=BF)[None, :, None, :]
     wide = (right_factor.transpose(1, 0, 2)[:, :, :, None] * same).reshape(nb * pos, nb * pos)
     wide_t = (right_factor.transpose(2, 0, 1)[:, :, :, None] * same).reshape(nb * pos, nb * pos)
+    sloped = grad_hidden * slope
+    moved, activated, sloped = lax.optimization_barrier((moved, activated, sloped))
     right_shape = jax.ShapeDtypeStruct((nb * pos, 128), BF)
     sent, term_right = in_vmem(middle_body, (pair, right_shape), moved, wide, wide_t)
     back = swap(sent, CTX)
@@ -170,7 +172,7 @@
     yc = lax.axis_size(YC)
     mixed = back[:, :pos].reshape(tok, ch).astype(F32)
     hidden = (mixed * activated).astype(BF)
-    grad_gate_pre = (grad_hidden * mixed * slope).astype(BF)
+    grad_gate_pre = (mixed * sloped).astype(BF)
 
     def by_yc(term):
         return term.astype(BF).reshape(nz, yc, nl // 2, -1, ch).transpose(1, 2, 0, 3, 4)

time: 211 us -> 210 us (level)
  waiting for transfers between devices: 52.2 us -> 47.8 us
    all_to_all x4, waiting for transfers between devices: 50.5 us -> 46.2 us  [swap(): return lax.all_to_all(blocks, axes, 0, 0, tiled=True)]
  transfers between devices with their start and end apart: 10 -> 10, of which waited for: 5 -> 5; matrix products, arithmetic and copies ran while one was open for 15% -> 16% of each run, Pallas kernels for 0% -> 0%
where the time goes in v5:
time: 210 us; the launch traced here: 209 us
  blocking collectives  60.7 us (29%)
  starting transfers between devices  54.5 us (26%)
  waiting for transfers between devices  47.8 us (23%)
  local copies, waits for them, and re-layouts  18 us (9%)
  other arithmetic  10.4 us (5%)
  matrix products  8.82 us (4%)
  Pallas kernels  7.63 us (4%)
    all_to_all x1, blocking collectives, swap(): return lax.all_to_all(blocks, axes, 0, 0, tiled=True)  60.7 us
    all_to_all x4, waiting for transfers between devices, swap(): return lax.all_to_all(blocks, axes, 0, 0, tiled=True)  46.2 us
    all_to_all x4, starting transfers between devices, swap(): return lax.all_to_all(blocks, axes, 0, 0, tiled=True)  32.9 us
    ppermute x6, starting transfers between devices, shift(): return lax.ppermute(block, axis, [(i, (i + step) % n) for i in range(n)])  21.6 us
    mul x1, local copies, waits for them, and re-layouts, per_device(): right_factor.transpose(1, 0, 2)[:, :, :, None] * same  7.86 us
    mul x1, local copies, waits for them, and re-layouts, per_device(): right_factor.transpose(2, 0, 1)[:, :, :, None] * same  7.78 us
    mul x1, other arithmetic, per_device(): right_factor.transpose(2, 0, 1)[:, :, :, None] * same  7.13 us
  transfers between devices with their start and end apart: 10, of which 5 were waited for; matrix products, arithmetic and copies ran while one was open for 16% of the time, Pallas kernels for 0%

profile of v5, /device:TPU:32, one launch (start us, length us, event | category | flops | bytes accessed | tf_op | source)
XLA Modules:
  0.0 208.7 jit_solution(1410280695231736255)
XLA Ops:
  0.6 3.5 %shard_map.109 = bf16[32,32,512]{2,1,0:T(8,128)(2,1)} custom-call(bf16[512,512]{1,0:T(8,128)(2,1)} %bitcast.94, bf16[512,512]{1,0:T(8,128)(2,1)} %bitcast.88, bf16[512,512]{1,0:T(8,128)(2,1)} %refs_2_.1, bf16[512,512]{1,0:T(8,128)(2,1)} %bitcast.98, bf16[512,512]{1,0:T(8,128)(2,1)} %refs_4_.1), custom_call_target="tpu_custom_call" | custom-call | tf_op jit(solution)/shard_map/pallas_call | solution.py:75
  4.1 17.2 %all-to-all-start = ((bf16[32,32,512]{2,1,0:T(8,128)(2,1)}), bf16[32,32,512]{2,1,0:T(8,128)(2,1)S(1)}, u32[]{:S(2)}, u32[]{:S(2)}) async-start(bf16[32,32,512]{2,1,0:T(8,128)(2,1)} %shard_map.109), calls=%async_computation | async-start | bytes 2097152 | tf_op jit(solution)/shard_map/all_to_all | solution.py:31
  21.6 7.1 %broadcast_multiply_fusion = (bf16[32,16,32,16]{3,2,1,0:T(8,128)(2,1)}, bf16[32,16,32,16]{3,2,1,0:T(8,128)(2,1)}) fusion(bf16[32,16,32]{2,1,0:T(8,128)(2,1)S(1)} %copy.20, bf16[16,16]{1,0:T(8,128)(2,1)S(1)} %fusion.17, bf16[32,16,32]{2,1,0:T(8,128)(2,1)S(1)} %copy.19), kind=kLoop, calls=%fused_computation | loop fusion | flops 524288 | bytes 1114624 | tf_op jit(solution)/shard_map/mul | solution.py:162
  28.8 7.9 %mul.59.wide = bf16[512,512]{1,0:T(8,128)(2,1)S(1)} reshape(bf16[32,16,32,16]{3,2,1,0:T(8,128)(2,1)} %get-tuple-element.48) | data formatting | bytes 1048576 | tf_op jit(solution)/shard_map/mul | solution.py:161
  36.6 7.8 %mul.62.wide_t = bf16[512,512]{1,0:T(8,128)(2,1)S(1)} reshape(bf16[32,16,32,16]{3,2,1,0:T(8,128)(2,1)} %get-tuple-element.47) | data formatting | bytes 1048576 | tf_op jit(solution)/shard_map/mul | solution.py:162
  44.5 1.6 fusion.5
  46.0 1.6 convolution_multiply_fusion
  47.6 28.8 %all-to-all-done.moved = bf16[32,32,512]{2,1,0:T(8,128)(2,1)S(1)} async-done(((bf16[32,32,512]{2,1,0:T(8,128)(2,1)}), bf16[32,32,512]{2,1,0:T(8,128)(2,1)S(1)}, u32[]{:S(2)}, u32[]{:S(2)}) %all-to-all-start) | async-done | bytes 1048608 | tf_op jit(solution)/shard_map/all_to_all | solution.py:31
  76.4 1.2 shard_map.110
  77.7 60.7 %all_to_all.25 = bf16[32,32,512]{2,1,0:T(8,128)(2,1)S(1)} all-to-all(bf16[32,32,512]{2,1,0:T(8,128)(2,1)S(1)} %get-tuple-element.16), channel_id=1, replica_groups=mesh['zl'=4,'x'=4,'zh'=4,'y'=4,'c'=2] {'zh','y','c'}, dimensions={0} | all-to-all | bytes 2097152 | tf_op jit(solution)/shard_map/all_to_all | solution.py:31
  138.8 0.8 copy-done.4
  140.7 1.1 pad_maximum_fusion
  141.8 5.3 %all-to-all-start.2 = ((bf16[8,128,512]{2,1,0:T(8,128)(2,1)}), bf16[8,128,512]{2,1,0:T(8,128)(2,1)S(1)}, u32[]{:S(2)}, u32[]{:S(2)}) async-start(bf16[8,128,512]{2,1,0:T(8,128)(2,1)} %bitcast.93), calls=%async_computation.2 | async-start | bytes 2097152 | tf_op jit(solution)/shard_map/all_to_all | solution.py:31
  148.4 2.2 %collective-permute-start.2 = (bf16[4,40,512]{2,1,0:T(8,128)(2,1)}, bf16[4,40,512]{2,1,0:T(8,128)(2,1)S(1)}, u32[]{:S(2)}, u32[]{:S(2)}) collective-permute-start(bf16[4,40,512]{2,1,0:T(8,128)(2,1)} %get-tuple-element.40), channel_id=1, source_target_pairs={{0,32},{32,64},{64,96},{96,0},{1,33},{33,65},{65,97},{97,1},{2,34}... | collective-permute-start | bytes 491528 | tf_op jit(solution)/shard_map/ppermute | solution.py:36
  150.6 5.8 %collective-permute-start.1 = (bf16[4,40,512]{2,1,0:T(8,128)(2,1)S(1)}, bf16[4,40,512]{2,1,0:T(8,128)(2,1)}, u32[]{:S(2)}, u32[]{:S(2)}) collective-permute-start(bf16[4,40,512]{2,1,0:T(8,128)(2,1)S(1)} %get-tuple-element.39), channel_id=1, source_target_pairs={{0,64},{32,96},{64,0},{96,32},{1,65},{33,97},{65,1},{97,33},{2,66}... | collective-permute-start | bytes 491528 | tf_op jit(solution)/shard_map/ppermute | solution.py:36
  156.4 2.6 %collective-permute-start = (bf16[4,40,512]{2,1,0:T(8,128)(2,1)S(1)}, bf16[4,40,512]{2,1,0:T(8,128)(2,1)}, u32[]{:S(2)}, u32[]{:S(2)}) collective-permute-start(bf16[4,40,512]{2,1,0:T(8,128)(2,1)S(1)} %get-tuple-element.38), channel_id=1, source_target_pairs={{0,96},{32,0},{64,32},{96,64},{1,97},{33,1},{65,33},{97,65},{2,98}... | collective-permute-start | bytes 491528 | tf_op jit(solution)/shard_map/ppermute | solution.py:36
  159.0 4.1 %all-to-all-done.2.parts = bf16[8,128,512]{2,1,0:T(8,128)(2,1)S(1)} async-done(((bf16[8,128,512]{2,1,0:T(8,128)(2,1)}), bf16[8,128,512]{2,1,0:T(8,128)(2,1)S(1)}, u32[]{:S(2)}, u32[]{:S(2)}) %all-to-all-start.2) | async-done | bytes 1048608 | tf_op jit(solution)/shard_map/all_to_all | solution.py:31
  163.1 0.8 shard_map.111
  163.9 3.5 %all-to-all-start.3 = ((bf16[16,8,512]{2,1,0:T(8,128)(2,1)}), bf16[16,8,512]{2,1,0:T(8,128)(2,1)S(1)}, u32[]{:S(2)}, u32[]{:S(2)}) async-start(bf16[16,8,512]{2,1,0:T(8,128)(2,1)} %bitcast.30), calls=%async_computation.3 | async-start | bytes 262144 | tf_op jit(solution)/shard_map/all_to_all | solution.py:31
  167.4 1.1 fusion.8
  168.5 2.1 collective-permute-start.3
  170.6 4.7 %collective-permute-start.4 = (bf16[40,512]{1,0:T(8,128)(2,1)S(1)}, bf16[40,512]{1,0:T(8,128)(2,1)S(1)}, u32[]{:S(2)}, u32[]{:S(2)}) collective-permute-start(bf16[40,512]{1,0:T(8,128)(2,1)S(1)} %get-tuple-element.44), channel_id=1, source_target_pairs={{0,256},{128,384},{256,0},{384,128},{1,257},{129,385},{257,1},{385... | collective-permute-start | bytes 122888 | tf_op jit(solution)/shard_map/ppermute | solution.py:36
  175.3 4.3 %collective-permute-start.5 = (bf16[40,512]{1,0:T(8,128)(2,1)S(1)}, bf16[40,512]{1,0:T(8,128)(2,1)S(1)}, u32[]{:S(2)}, u32[]{:S(2)}) collective-permute-start(bf16[40,512]{1,0:T(8,128)(2,1)S(1)} %get-tuple-element.43), channel_id=1, source_target_pairs={{0,128},{128,256},{256,384},{384,0},{1,129},{129,257},{257,385},{3... | collective-permute-start | bytes 122888 | tf_op jit(solution)/shard_map/ppermute | solution.py:36
  179.6 1.6 collective-permute-done.5.three
  181.7 1.0 shard_map.112
  182.7 6.8 %all-to-all-start.4 = ((bf16[16,48,512]{2,1,0:T(8,128)(2,1)}), bf16[16,48,512]{2,1,0:T(8,128)(2,1)S(1)}, u32[]{:S(2)}, u32[]{:S(2)}) async-start(bf16[16,48,512]{2,1,0:T(8,128)(2,1)} %shard_map.112), calls=%async_computation.4 | async-start | bytes 1572864 | tf_op jit(solution)/shard_map/all_to_all | solution.py:31
  189.5 1.5 convolution_bitcast_fusion
  191.0 1.5 fusion.1
  192.5 1.0 copy.27
  193.5 1.2 fusion.2
  194.8 12.8 %all-to-all-done.4.packed = bf16[16,48,512]{2,1,0:T(8,128)(2,1)S(1)} async-done(((bf16[16,48,512]{2,1,0:T(8,128)(2,1)}), bf16[16,48,512]{2,1,0:T(8,128)(2,1)S(1)}, u32[]{:S(2)}, u32[]{:S(2)}) %all-to-all-start.4) | async-done | bytes 786464 | tf_op jit(solution)/shard_map/all_to_all | solution.py:31
  207.6 1.1 shard_map.113
  (39 shorter events, 3.5 us)
Async XLA Ops:
  0.6 20.7 %copy-start.10 = (bf16[16,32,32]{2,1,0:T(8,128)(2,1)S(1)}, bf16[16,32,32]{2,1,0:T(8,128)(2,1)}, u32[]{:S(2)}) copy-start(bf16[16,32,32]{2,1,0:T(8,128)(2,1)} %param.11) | copy-start | bytes 98308
  4.1 72.3 %all-to-all-start = ((bf16[32,32,512]{2,1,0:T(8,128)(2,1)}), bf16[32,32,512]{2,1,0:T(8,128)(2,1)S(1)}, u32[]{:S(2)}, u32[]{:S(2)}) async-start(bf16[32,32,512]{2,1,0:T(8,128)(2,1)} %shard_map.109), calls=%async_computation | async-start | bytes 2097152 | tf_op jit(solution)/shard_map/all_to_all | solution.py:31
  28.8 15.7 %copy-start = (bf16[1,512,512]{2,1,0:T(8,128)(2,1)S(1)}, bf16[1,512,512]{2,1,0:T(8,128)(2,1)}, u32[]{:S(2)}) copy-start(bf16[1,512,512]{2,1,0:T(8,128)(2,1)} %param.6) | copy-start | bytes 1572868
  28.8 15.7 %copy-start.1 = (bf16[512,512]{1,0:T(8,128)(2,1)S(1)}, bf16[512,512]{1,0:T(8,128)(2,1)}, u32[]{:S(2)}) copy-start(bf16[512,512]{1,0:T(8,128)(2,1)} %refs_2_.1) | copy-start | bytes 1572868
  44.4 1.6 copy-start.2
  44.5 1.6 copy-start.8
  76.4 62.0 %copy-start.6 = (f32[512,512]{1,0:T(8,128)S(1)}, f32[512,512]{1,0:T(8,128)}, u32[]{:S(2)}) copy-start(f32[512,512]{1,0:T(8,128)} %get-tuple-element.17) | copy-start | bytes 3145732
  76.4 62.0 %copy-start.7 = (f32[512,512]{1,0:T(8,128)S(1)}, f32[512,512]{1,0:T(8,128)}, u32[]{:S(2)}) copy-start(f32[512,512]{1,0:T(8,128)} %convolution_multiply_fusion) | copy-start | bytes 3145732
  77.7 61.9 %copy-start.9 = (bf16[1,512,512]{2,1,0:T(8,128)(2,1)S(1)}, bf16[1,512,512]{2,1,0:T(8,128)(2,1)}, u32[]{:S(2)}) copy-start(bf16[1,512,512]{2,1,0:T(8,128)(2,1)} %param.7) | copy-start | bytes 1572868
  138.8 0.8 copy-start.4
  141.8 21.3 %all-to-all-start.2 = ((bf16[8,128,512]{2,1,0:T(8,128)(2,1)}), bf16[8,128,512]{2,1,0:T(8,128)(2,1)S(1)}, u32[]{:S(2)}, u32[]{:S(2)}) async-start(bf16[8,128,512]{2,1,0:T(8,128)(2,1)} %bitcast.93), calls=%async_computation.2 | async-start | bytes 2097152 | tf_op jit(solution)/shard_map/all_to_all | solution.py:31
  148.4 19.0 %collective-permute-start.2 = (bf16[4,40,512]{2,1,0:T(8,128)(2,1)}, bf16[4,40,512]{2,1,0:T(8,128)(2,1)S(1)}, u32[]{:S(2)}, u32[]{:S(2)}) collective-permute-start(bf16[4,40,512]{2,1,0:T(8,128)(2,1)} %get-tuple-element.40), channel_id=1, source_target_pairs={{0,32},{32,64},{64,96},{96,0},{1,33},{33,65},{65,97},{97,1},{2,34}... | collective-permute-start | bytes 491528 | tf_op jit(solution)/shard_map/ppermute | solution.py:36
  150.6 16.8 %collective-permute-start.1 = (bf16[4,40,512]{2,1,0:T(8,128)(2,1)S(1)}, bf16[4,40,512]{2,1,0:T(8,128)(2,1)}, u32[]{:S(2)}, u32[]{:S(2)}) collective-permute-start(bf16[4,40,512]{2,1,0:T(8,128)(2,1)S(1)} %get-tuple-element.39), channel_id=1, source_target_pairs={{0,64},{32,96},{64,0},{96,32},{1,65},{33,97},{65,1},{97,33},{2,66}... | collective-permute-start | bytes 491528 | tf_op jit(solution)/shard_map/ppermute | solution.py:36
  156.4 11.0 %collective-permute-start = (bf16[4,40,512]{2,1,0:T(8,128)(2,1)S(1)}, bf16[4,40,512]{2,1,0:T(8,128)(2,1)}, u32[]{:S(2)}, u32[]{:S(2)}) collective-permute-start(bf16[4,40,512]{2,1,0:T(8,128)(2,1)S(1)} %get-tuple-element.38), channel_id=1, source_target_pairs={{0,96},{32,0},{64,32},{96,64},{1,97},{33,1},{65,33},{97,65},{2,98}... | collective-permute-start | bytes 491528 | tf_op jit(solution)/shard_map/ppermute | solution.py:36
  163.9 17.8 %all-to-all-start.3 = ((bf16[16,8,512]{2,1,0:T(8,128)(2,1)}), bf16[16,8,512]{2,1,0:T(8,128)(2,1)S(1)}, u32[]{:S(2)}, u32[]{:S(2)}) async-start(bf16[16,8,512]{2,1,0:T(8,128)(2,1)} %bitcast.30), calls=%async_computation.3 | async-start | bytes 262144 | tf_op jit(solution)/shard_map/all_to_all | solution.py:31
  168.5 11.0 %collective-permute-start.3 = (bf16[40,512]{1,0:T(8,128)(2,1)S(1)}, bf16[40,512]{1,0:T(8,128)(2,1)S(1)}, u32[]{:S(2)}, u32[]{:S(2)}) collective-permute-start(bf16[40,512]{1,0:T(8,128)(2,1)S(1)} %get-tuple-element.45), channel_id=1, source_target_pairs={{0,384},{128,0},{256,128},{384,256},{1,385},{129,1},{257,129},{385... | collective-permute-start | bytes 122888 | tf_op jit(solution)/shard_map/ppermute | solution.py:36
  170.6 9.0 %collective-permute-start.4 = (bf16[40,512]{1,0:T(8,128)(2,1)S(1)}, bf16[40,512]{1,0:T(8,128)(2,1)S(1)}, u32[]{:S(2)}, u32[]{:S(2)}) collective-permute-start(bf16[40,512]{1,0:T(8,128)(2,1)S(1)} %get-tuple-element.44), channel_id=1, source_target_pairs={{0,256},{128,384},{256,0},{384,128},{1,257},{129,385},{257,1},{385... | collective-permute-start | bytes 122888 | tf_op jit(solution)/shard_map/ppermute | solution.py:36
  175.3 5.9 %collective-permute-start.5 = (bf16[40,512]{1,0:T(8,128)(2,1)S(1)}, bf16[40,512]{1,0:T(8,128)(2,1)S(1)}, u32[]{:S(2)}, u32[]{:S(2)}) collective-permute-start(bf16[40,512]{1,0:T(8,128)(2,1)S(1)} %get-tuple-element.43), channel_id=1, source_target_pairs={{0,128},{128,256},{256,384},{384,0},{1,129},{129,257},{257,385},{3... | collective-permute-start | bytes 122888 | tf_op jit(solution)/shard_map/ppermute | solution.py:36
  181.7 11.8 %copy-start.3 = (bf16[512,512]{1,0:T(8,128)(2,1)S(1)}, bf16[512,512]{1,0:T(8,128)(2,1)}, u32[]{:S(2)}) copy-start(bf16[512,512]{1,0:T(8,128)(2,1)} %refs_4_.1) | copy-start | bytes 1572868
  181.7 11.8 %copy-start.5 = (bf16[512,512]{1,0:T(8,128)(2,1)S(1)}, bf16[512,512]{1,0:T(8,128)(2,1)}, u32[]{:S(2)}) copy-start(bf16[512,512]{1,0:T(8,128)(2,1)} %copy-done.4) | copy-start | bytes 1572868
  182.7 24.9 %all-to-all-start.4 = ((bf16[16,48,512]{2,1,0:T(8,128)(2,1)}), bf16[16,48,512]{2,1,0:T(8,128)(2,1)S(1)}, u32[]{:S(2)}, u32[]{:S(2)}) async-start(bf16[16,48,512]{2,1,0:T(8,128)(2,1)} %shard_map.112), calls=%async_computation.4 | async-start | bytes 1572864 | tf_op jit(solution)/shard_map/all_to_all | solution.py:31

commit v6 on v5

--- a/solution.py
+++ b/solution.py
@@ -110,6 +110,15 @@
     right[...] = mm(kept, choose).astype(BF)
 
 
+def terms_body(x, grad_gate_pre, hidden, cot, terms):
+    yc, nl, nz, part, ch = terms.shape
+    for i, term in enumerate((mm_tl(x[...], grad_gate_pre[...]), mm_tl(hidden[...], cot[...]))):
+        term = term.reshape(nz, yc, nl // 2, part, ch)
+        for half in range(nl // 2):
+            for z in range(nz):
+                terms[:, i * (nl // 2) + half, z] = term[z, :, half].astype(BF)
+
+
 def sum_body(parts, total):
     total[...] = parts[...].astype(F32).sum(0).astype(BF)
 
@@ -174,10 +183,8 @@
     hidden = (mixed * activated).astype(BF)
     grad_gate_pre = (mixed * sloped).astype(BF)
 
-    def by_yc(term):
-        return term.astype(BF).reshape(nz, yc, nl // 2, -1, ch).transpose(1, 2, 0, 3, 4)
-
-    terms = jnp.concatenate([by_yc(mm_tl(x, grad_gate_pre)), by_yc(mm_tl(hidden, cot))], 1)
+    laid = jax.ShapeDtypeStruct((yc, nl, nz, 2 * share // nl, ch), BF)
+    terms = in_vmem(terms_body, laid, x, grad_gate_pre, hidden, cot)
     initial_gradient = back[:, pos:].reshape(tok, ch)
 
     terms = swap(terms.reshape(yc, nz * 2 * share, ch), YC)

time: 210 us -> 209 us (level)
  waiting for transfers between devices: 47.8 us -> 45.4 us
    all_to_all x4, waiting for transfers between devices: 46.2 us -> 43.8 us  [swap(): return lax.all_to_all(blocks, axes, 0, 0, tiled=True)]
    pallas_call x4 -> x5, Pallas kernels: 4.14 us -> 5.84 us  [in_vmem(): pl.pallas_call(body, out_shape=out_shape, in_specs=[vmem] * len(args), ou...]
  transfers between devices with their start and end apart: 10 -> 10, of which waited for: 5 -> 5; matrix products, arithmetic and copies ran while one was open for 16% -> 17% of each run, Pallas kernels for 0% -> 0%
where the time goes in v6:
time: 209 us; the launch traced here: 208 us
  blocking collectives  60.6 us (29%)
  starting transfers between devices  54.6 us (26%)
  waiting for transfers between devices  45.4 us (22%)
  local copies, waits for them, and re-layouts  17.9 us (9%)
  matrix products  10.2 us (5%)
  Pallas kernels  9.38 us (4%)
  other arithmetic  9.32 us (4%)
    all_to_all x1, blocking collectives, swap(): return lax.all_to_all(blocks, axes, 0, 0, tiled=True)  60.6 us
    all_to_all x4, waiting for transfers between devices, swap(): return lax.all_to_all(blocks, axes, 0, 0, tiled=True)  43.8 us
    all_to_all x4, starting transfers between devices, swap(): return lax.all_to_all(blocks, axes, 0, 0, tiled=True)  32.9 us
    ppermute x6, starting transfers between devices, shift(): return lax.ppermute(block, axis, [(i, (i + step) % n) for i in range(n)])  21.6 us
    mul x1, local copies, waits for them, and re-layouts, per_device(): right_factor.transpose(2, 0, 1)[:, :, :, None] * same  7.84 us
    mul x1, local copies, waits for them, and re-layouts, per_device(): right_factor.transpose(1, 0, 2)[:, :, :, None] * same  7.83 us
    mul x1, other arithmetic, per_device(): right_factor.transpose(2, 0, 1)[:, :, :, None] * same  7.15 us
    pallas_call x5, Pallas kernels, in_vmem(): pl.pallas_call(body, out_shape=out_shape, in_specs=[vmem] * len(args), ou...  5.84 us
  transfers between devices with their start and end apart: 10, of which 5 were waited for; matrix products, arithmetic and copies ran while one was open for 17% of the time, Pallas kernels for 0%

profile of v6, /device:TPU:32, one launch (start us, length us, event | category | flops | bytes accessed | tf_op | source)
XLA Modules:
  0.0 208.2 jit_solution(17236948147039990738)
XLA Ops:
  0.6 3.5 %shard_map.109 = bf16[32,32,512]{2,1,0:T(8,128)(2,1)} custom-call(bf16[512,512]{1,0:T(8,128)(2,1)} %bitcast.82, bf16[512,512]{1,0:T(8,128)(2,1)} %bitcast.73, bf16[512,512]{1,0:T(8,128)(2,1)} %refs_2_.1, bf16[512,512]{1,0:T(8,128)(2,1)} %bitcast.75, bf16[512,512]{1,0:T(8,128)(2,1)} %refs_4_.1), custom_call_target="tpu_custom_call" | custom-call | tf_op jit(solution)/shard_map/pallas_call | solution.py:75
  4.2 17.2 %all-to-all-start = ((bf16[32,32,512]{2,1,0:T(8,128)(2,1)}), bf16[32,32,512]{2,1,0:T(8,128)(2,1)S(1)}, u32[]{:S(2)}, u32[]{:S(2)}) async-start(bf16[32,32,512]{2,1,0:T(8,128)(2,1)} %shard_map.109), calls=%async_computation | async-start | bytes 2097152 | tf_op jit(solution)/shard_map/all_to_all | solution.py:31
  21.7 7.2 %broadcast_multiply_fusion = (bf16[32,16,32,16]{3,2,1,0:T(8,128)(2,1)}, bf16[32,16,32,16]{3,2,1,0:T(8,128)(2,1)}) fusion(bf16[32,16,32]{2,1,0:T(8,128)(2,1)S(1)} %copy.18, bf16[16,16]{1,0:T(8,128)(2,1)S(1)} %fusion.17, bf16[32,16,32]{2,1,0:T(8,128)(2,1)S(1)} %copy.17), kind=kLoop, calls=%fused_computation | loop fusion | flops 524288 | bytes 1114624 | tf_op jit(solution)/shard_map/mul | solution.py:171
  28.8 7.8 %mul.59.wide = bf16[512,512]{1,0:T(8,128)(2,1)S(1)} reshape(bf16[32,16,32,16]{3,2,1,0:T(8,128)(2,1)} %get-tuple-element.48) | data formatting | bytes 1048576 | tf_op jit(solution)/shard_map/mul | solution.py:170
  36.7 7.8 %mul.62.wide_t = bf16[512,512]{1,0:T(8,128)(2,1)S(1)} reshape(bf16[32,16,32,16]{3,2,1,0:T(8,128)(2,1)} %get-tuple-element.47) | data formatting | bytes 1048576 | tf_op jit(solution)/shard_map/mul | solution.py:171
  44.5 2.7 %fusion.5 = (f32[512,512]{1,0:T(8,128)}, f32[512,512]{1,0:T(8,128)S(1)}) fusion(bf16[512,512]{1,0:T(8,128)(2,1)} %refs_2_.1, bf16[1,512,512]{2,1,0:T(8,128)(2,1)S(1)} %copy-done), kind=kOutput, calls=%fused_computation.19 | convolution fusion | flops 269484032 | bytes 3145728 | tf_op jit(solution)/shard_map/dot_general | solution.py:19
  47.2 1.7 convolution_multiply_fusion
  48.9 27.6 %all-to-all-done.moved = bf16[32,32,512]{2,1,0:T(8,128)(2,1)S(1)} async-done(((bf16[32,32,512]{2,1,0:T(8,128)(2,1)}), bf16[32,32,512]{2,1,0:T(8,128)(2,1)S(1)}, u32[]{:S(2)}, u32[]{:S(2)}) %all-to-all-start) | async-done | bytes 1048608 | tf_op jit(solution)/shard_map/all_to_all | solution.py:31
  76.5 1.2 shard_map.110
  77.7 60.6 %all_to_all.25 = bf16[32,32,512]{2,1,0:T(8,128)(2,1)S(1)} all-to-all(bf16[32,32,512]{2,1,0:T(8,128)(2,1)S(1)} %get-tuple-element.16), channel_id=1, replica_groups=mesh['zl'=4,'x'=4,'zh'=4,'y'=4,'c'=2] {'zh','y','c'}, dimensions={0} | all-to-all | bytes 2097152 | tf_op jit(solution)/shard_map/all_to_all | solution.py:31
  138.3 0.9 fusion.23
  139.5 1.7 shard_map.111
  141.2 5.3 %all-to-all-start.2 = ((bf16[8,128,512]{2,1,0:T(8,128)(2,1)}), bf16[8,128,512]{2,1,0:T(8,128)(2,1)S(1)}, u32[]{:S(2)}, u32[]{:S(2)}) async-start(bf16[8,128,512]{2,1,0:T(8,128)(2,1)} %bitcast.24), calls=%async_computation.2 | async-start | bytes 2097152 | tf_op jit(solution)/shard_map/all_to_all | solution.py:31
  146.6 1.5 convolution_convert_fusion
  148.8 2.3 %collective-permute-start.2 = (bf16[4,40,512]{2,1,0:T(8,128)(2,1)}, bf16[4,40,512]{2,1,0:T(8,128)(2,1)S(1)}, u32[]{:S(2)}, u32[]{:S(2)}) collective-permute-start(bf16[4,40,512]{2,1,0:T(8,128)(2,1)} %get-tuple-element.40), channel_id=1, source_target_pairs={{0,32},{32,64},{64,96},{96,0},{1,33},{33,65},{65,97},{97,1},{2,34}... | collective-permute-start | bytes 491528 | tf_op jit(solution)/shard_map/ppermute | solution.py:36
  151.1 5.8 %collective-permute-start.1 = (bf16[4,40,512]{2,1,0:T(8,128)(2,1)S(1)}, bf16[4,40,512]{2,1,0:T(8,128)(2,1)}, u32[]{:S(2)}, u32[]{:S(2)}) collective-permute-start(bf16[4,40,512]{2,1,0:T(8,128)(2,1)S(1)} %get-tuple-element.39), channel_id=1, source_target_pairs={{0,64},{32,96},{64,0},{96,32},{1,65},{33,97},{65,1},{97,33},{2,66}... | collective-permute-start | bytes 491528 | tf_op jit(solution)/shard_map/ppermute | solution.py:36
  156.9 2.6 %collective-permute-start = (bf16[4,40,512]{2,1,0:T(8,128)(2,1)S(1)}, bf16[4,40,512]{2,1,0:T(8,128)(2,1)}, u32[]{:S(2)}, u32[]{:S(2)}) collective-permute-start(bf16[4,40,512]{2,1,0:T(8,128)(2,1)S(1)} %get-tuple-element.38), channel_id=1, source_target_pairs={{0,96},{32,0},{64,32},{96,64},{1,97},{33,1},{65,33},{97,65},{2,98}... | collective-permute-start | bytes 491528 | tf_op jit(solution)/shard_map/ppermute | solution.py:36
  159.5 3.0 %all-to-all-done.2.parts = bf16[8,128,512]{2,1,0:T(8,128)(2,1)S(1)} async-done(((bf16[8,128,512]{2,1,0:T(8,128)(2,1)}), bf16[8,128,512]{2,1,0:T(8,128)(2,1)S(1)}, u32[]{:S(2)}, u32[]{:S(2)}) %all-to-all-start.2) | async-done | bytes 1048608 | tf_op jit(solution)/shard_map/all_to_all | solution.py:31
  163.3 3.5 %all-to-all-start.3 = ((bf16[16,8,512]{2,1,0:T(8,128)(2,1)}), bf16[16,8,512]{2,1,0:T(8,128)(2,1)S(1)}, u32[]{:S(2)}, u32[]{:S(2)}) async-start(bf16[16,8,512]{2,1,0:T(8,128)(2,1)} %bitcast.25), calls=%async_computation.3 | async-start | bytes 262144 | tf_op jit(solution)/shard_map/all_to_all | solution.py:31
  166.8 1.1 fusion.8
  168.0 2.1 collective-permute-start.3
  170.0 4.7 %collective-permute-start.4 = (bf16[40,512]{1,0:T(8,128)(2,1)S(1)}, bf16[40,512]{1,0:T(8,128)(2,1)S(1)}, u32[]{:S(2)}, u32[]{:S(2)}) collective-permute-start(bf16[40,512]{1,0:T(8,128)(2,1)S(1)} %get-tuple-element.44), channel_id=1, source_target_pairs={{0,256},{128,384},{256,0},{384,128},{1,257},{129,385},{257,1},{385... | collective-permute-start | bytes 122888 | tf_op jit(solution)/shard_map/ppermute | solution.py:36
  174.7 4.3 %collective-permute-start.5 = (bf16[40,512]{1,0:T(8,128)(2,1)S(1)}, bf16[40,512]{1,0:T(8,128)(2,1)S(1)}, u32[]{:S(2)}, u32[]{:S(2)}) collective-permute-start(bf16[40,512]{1,0:T(8,128)(2,1)S(1)} %get-tuple-element.43), channel_id=1, source_target_pairs={{0,128},{128,256},{256,384},{384,0},{1,129},{129,257},{257,385},{3... | collective-permute-start | bytes 122888 | tf_op jit(solution)/shard_map/ppermute | solution.py:36
  179.0 1.6 collective-permute-done.5.three
  181.1 1.0 shard_map.113
  182.1 6.8 %all-to-all-start.4 = ((bf16[16,48,512]{2,1,0:T(8,128)(2,1)}), bf16[16,48,512]{2,1,0:T(8,128)(2,1)S(1)}, u32[]{:S(2)}, u32[]{:S(2)}) async-start(bf16[16,48,512]{2,1,0:T(8,128)(2,1)} %shard_map.113), calls=%async_computation.4 | async-start | bytes 1572864 | tf_op jit(solution)/shard_map/all_to_all | solution.py:31
  188.9 1.7 convolution_bitcast_fusion
  190.6 1.5 fusion.1
  192.1 1.0 copy.23
  193.1 1.2 fusion.2
  194.4 12.7 %all-to-all-done.4.packed = bf16[16,48,512]{2,1,0:T(8,128)(2,1)S(1)} async-done(((bf16[16,48,512]{2,1,0:T(8,128)(2,1)}), bf16[16,48,512]{2,1,0:T(8,128)(2,1)S(1)}, u32[]{:S(2)}, u32[]{:S(2)}) %all-to-all-start.4) | async-done | bytes 786464 | tf_op jit(solution)/shard_map/all_to_all | solution.py:31
  207.1 1.1 shard_map.114
  (28 shorter events, 2.7 us)
Async XLA Ops:
  0.6 20.8 %copy-start.6 = (bf16[16,32,32]{2,1,0:T(8,128)(2,1)S(1)}, bf16[16,32,32]{2,1,0:T(8,128)(2,1)}, u32[]{:S(2)}) copy-start(bf16[16,32,32]{2,1,0:T(8,128)(2,1)} %param.11) | copy-start | bytes 98308
  4.2 72.3 %all-to-all-start = ((bf16[32,32,512]{2,1,0:T(8,128)(2,1)}), bf16[32,32,512]{2,1,0:T(8,128)(2,1)S(1)}, u32[]{:S(2)}, u32[]{:S(2)}) async-start(bf16[32,32,512]{2,1,0:T(8,128)(2,1)} %shard_map.109), calls=%async_computation | async-start | bytes 2097152 | tf_op jit(solution)/shard_map/all_to_all | solution.py:31
  28.8 15.7 %copy-start = (bf16[1,512,512]{2,1,0:T(8,128)(2,1)S(1)}, bf16[1,512,512]{2,1,0:T(8,128)(2,1)}, u32[]{:S(2)}) copy-start(bf16[1,512,512]{2,1,0:T(8,128)(2,1)} %param.6) | copy-start | bytes 1572868
  36.7 10.5 %copy-start.1 = (bf16[1,512,512]{2,1,0:T(8,128)(2,1)S(1)}, bf16[1,512,512]{2,1,0:T(8,128)(2,1)}, u32[]{:S(2)}) copy-start(bf16[1,512,512]{2,1,0:T(8,128)(2,1)} %param.7) | copy-start | bytes 1572868
  44.5 2.7 %copy-start.2 = (bf16[512,512]{1,0:T(8,128)(2,1)S(1)}, bf16[512,512]{1,0:T(8,128)(2,1)}, u32[]{:S(2)}) copy-start(bf16[512,512]{1,0:T(8,128)(2,1)} %refs_4_.1) | copy-start | bytes 1572868
  76.5 62.7 %copy-start.4 = (f32[512,512]{1,0:T(8,128)S(1)}, f32[512,512]{1,0:T(8,128)}, u32[]{:S(2)}) copy-start(f32[512,512]{1,0:T(8,128)} %get-tuple-element.17) | copy-start | bytes 3145732
  76.5 62.7 %copy-start.5 = (f32[512,512]{1,0:T(8,128)S(1)}, f32[512,512]{1,0:T(8,128)}, u32[]{:S(2)}) copy-start(f32[512,512]{1,0:T(8,128)} %convolution_multiply_fusion) | copy-start | bytes 3145732
  141.2 21.3 %all-to-all-start.2 = ((bf16[8,128,512]{2,1,0:T(8,128)(2,1)}), bf16[8,128,512]{2,1,0:T(8,128)(2,1)S(1)}, u32[]{:S(2)}, u32[]{:S(2)}) async-start(bf16[8,128,512]{2,1,0:T(8,128)(2,1)} %bitcast.24), calls=%async_computation.2 | async-start | bytes 2097152 | tf_op jit(solution)/shard_map/all_to_all | solution.py:31
  148.8 18.0 %collective-permute-start.2 = (bf16[4,40,512]{2,1,0:T(8,128)(2,1)}, bf16[4,40,512]{2,1,0:T(8,128)(2,1)S(1)}, u32[]{:S(2)}, u32[]{:S(2)}) collective-permute-start(bf16[4,40,512]{2,1,0:T(8,128)(2,1)} %get-tuple-element.40), channel_id=1, source_target_pairs={{0,32},{32,64},{64,96},{96,0},{1,33},{33,65},{65,97},{97,1},{2,34}... | collective-permute-start | bytes 491528 | tf_op jit(solution)/shard_map/ppermute | solution.py:36
  151.1 15.7 %collective-permute-start.1 = (bf16[4,40,512]{2,1,0:T(8,128)(2,1)S(1)}, bf16[4,40,512]{2,1,0:T(8,128)(2,1)}, u32[]{:S(2)}, u32[]{:S(2)}) collective-permute-start(bf16[4,40,512]{2,1,0:T(8,128)(2,1)S(1)} %get-tuple-element.39), channel_id=1, source_target_pairs={{0,64},{32,96},{64,0},{96,32},{1,65},{33,97},{65,1},{97,33},{2,66}... | collective-permute-start | bytes 491528 | tf_op jit(solution)/shard_map/ppermute | solution.py:36
  156.9 10.0 %collective-permute-start = (bf16[4,40,512]{2,1,0:T(8,128)(2,1)S(1)}, bf16[4,40,512]{2,1,0:T(8,128)(2,1)}, u32[]{:S(2)}, u32[]{:S(2)}) collective-permute-start(bf16[4,40,512]{2,1,0:T(8,128)(2,1)S(1)} %get-tuple-element.38), channel_id=1, source_target_pairs={{0,96},{32,0},{64,32},{96,64},{1,97},{33,1},{65,33},{97,65},{2,98}... | collective-permute-start | bytes 491528 | tf_op jit(solution)/shard_map/ppermute | solution.py:36
  163.3 17.8 %all-to-all-start.3 = ((bf16[16,8,512]{2,1,0:T(8,128)(2,1)}), bf16[16,8,512]{2,1,0:T(8,128)(2,1)S(1)}, u32[]{:S(2)}, u32[]{:S(2)}) async-start(bf16[16,8,512]{2,1,0:T(8,128)(2,1)} %bitcast.25), calls=%async_computation.3 | async-start | bytes 262144 | tf_op jit(solution)/shard_map/all_to_all | solution.py:31
  168.0 11.0 %collective-permute-start.3 = (bf16[40,512]{1,0:T(8,128)(2,1)S(1)}, bf16[40,512]{1,0:T(8,128)(2,1)S(1)}, u32[]{:S(2)}, u32[]{:S(2)}) collective-permute-start(bf16[40,512]{1,0:T(8,128)(2,1)S(1)} %get-tuple-element.45), channel_id=1, source_target_pairs={{0,384},{128,0},{256,128},{384,256},{1,385},{129,1},{257,129},{385... | collective-permute-start | bytes 122888 | tf_op jit(solution)/shard_map/ppermute | solution.py:36
  170.0 9.0 %collective-permute-start.4 = (bf16[40,512]{1,0:T(8,128)(2,1)S(1)}, bf16[40,512]{1,0:T(8,128)(2,1)S(1)}, u32[]{:S(2)}, u32[]{:S(2)}) collective-permute-start(bf16[40,512]{1,0:T(8,128)(2,1)S(1)} %get-tuple-element.44), channel_id=1, source_target_pairs={{0,256},{128,384},{256,0},{384,128},{1,257},{129,385},{257,1},{385... | collective-permute-start | bytes 122888 | tf_op jit(solution)/shard_map/ppermute | solution.py:36
  174.7 5.9 %collective-permute-start.5 = (bf16[40,512]{1,0:T(8,128)(2,1)S(1)}, bf16[40,512]{1,0:T(8,128)(2,1)S(1)}, u32[]{:S(2)}, u32[]{:S(2)}) collective-permute-start(bf16[40,512]{1,0:T(8,128)(2,1)S(1)} %get-tuple-element.43), channel_id=1, source_target_pairs={{0,128},{128,256},{256,384},{384,0},{1,129},{129,257},{257,385},{3... | collective-permute-start | bytes 122888 | tf_op jit(solution)/shard_map/ppermute | solution.py:36
  181.1 12.0 %copy-start.3 = (bf16[512,512]{1,0:T(8,128)(2,1)S(1)}, bf16[512,512]{1,0:T(8,128)(2,1)}, u32[]{:S(2)}) copy-start(bf16[512,512]{1,0:T(8,128)(2,1)} %refs_4_.1) | copy-start | bytes 1572868
  182.1 25.0 %all-to-all-start.4 = ((bf16[16,48,512]{2,1,0:T(8,128)(2,1)}), bf16[16,48,512]{2,1,0:T(8,128)(2,1)S(1)}, u32[]{:S(2)}, u32[]{:S(2)}) async-start(bf16[16,48,512]{2,1,0:T(8,128)(2,1)} %shard_map.113), calls=%async_computation.4 | async-start | bytes 1572864 | tf_op jit(solution)/shard_map/all_to_all | solution.py:31
